TPU v7x, 32 devices: a whole 2x2x4 slice. The times are simulated.
32 devices in a mesh: fsdp: 16 (over z, x, core), tensor: 2 (over y).
Axes of the slice: x: 2, y: 2, z: 4, core: 2. Of those that a mesh axis runs over, the one named last changes fastest.
Arguments:
- tokens: bfloat16 [16, 1024, 1024], P('fsdp', 'tensor'), may hold values from -6 to 6
- segments: int32 [16, 1024], P('fsdp'), may hold values from 0 to 14, as said below
- attn_gain: bfloat16 [1024], P('fsdp'), may hold values from 0.5 to 1.5
- mlp_gain: bfloat16 [1024], P('fsdp'), may hold values from 0.5 to 1.5
- query_gain: bfloat16 [128], P('fsdp'), may hold values from 0.25 to 1.75
- key_gain: bfloat16 [128], P('fsdp'), may hold values from 0.25 to 1.75
- query_weight: bfloat16 [1024, 2048], P('fsdp', 'tensor'), may hold values from -0.1875 to 0.1875
- key_matrix: bfloat16 [1024, 1024], P('fsdp', 'tensor'), may hold values from -0.1875 to 0.1875
- value_matrix: bfloat16 [1024, 1024], P('fsdp', 'tensor'), may hold values from -0.1875 to 0.1875
- output_weight: bfloat16 [2048, 1024], P('tensor', 'fsdp'), may hold values from -1 to 1
- gate_weight: bfloat16 [1024, 3072], P('fsdp', 'tensor'), may hold values from -0.1875 to 0.1875
- up_weight: bfloat16 [1024, 3072], P('fsdp', 'tensor'), may hold values from -0.1875 to 0.1875
- down_weight: bfloat16 [3072, 1024], P('tensor', 'fsdp'), may hold values from -0.109375 to 0.109375
- cotangent: bfloat16 [16, 1024, 1024], P('fsdp', 'tensor'), may hold values from -6 to 6
Outputs:
- layer_out: bfloat16 [16, 1024, 1024], P('fsdp', 'tensor')
- grad_tokens: float32 [16, 1024, 1024], P('fsdp', 'tensor')
- attn_gain_grad: float32 [1024], P('fsdp')
- mlp_gain_grad: float32 [1024], P('fsdp')
- query_gain_grad: float32 [128], P('fsdp')
- key_gain_grad: float32 [128], P('fsdp')
- query_grad: float32 [1024, 2048], P('fsdp', 'tensor')
- key_grad: float32 [1024, 1024], P('fsdp', 'tensor')
- value_grad: float32 [1024, 1024], P('fsdp', 'tensor')
- output_grad: float32 [2048, 1024], P('tensor', 'fsdp')
- gate_grad: float32 [1024, 3072], P('fsdp', 'tensor')
- up_grad: float32 [1024, 3072], P('fsdp', 'tensor')
- down_grad: float32 [3072, 1024], P('tensor', 'fsdp')
Inputs may be any that keep to these rules, and one draw needn't show every extreme that they name: `segments`: numbers the documents of each sequence from 0 upward in order, rising by one at each document start; every document starts at a multiple of 64 tokens.
All inputs are finite; a program needn't handle non-finite values.
Results may differ from a plain program's by a relative error of at most 0.014.
Values may be sent and summed in bfloat16 or wider, within the bound.
A program may use at most 256 MiB of HBM per device.

v0:
```python
import jax
import jax.numpy as jnp
from jax import lax
from jax.sharding import PartitionSpec as P

epsilon = 1e-06
rope_base = 1000000.0


def positions_of(segment_rows):
    seq_length = segment_rows.shape[-1]
    token_index = jnp.arange(seq_length, dtype=jnp.int32)
    change = jnp.concatenate(
        [
            jnp.ones(segment_rows.shape[:-1] + (1,), bool),
            segment_rows[..., 1:] != segment_rows[..., :-1],
        ],
        axis=-1,
    )
    begins = lax.cummax(jnp.where(change, token_index, 0), axis=segment_rows.ndim - 1)
    return token_index - begins


def rope_tables(positions, width):
    half_width = width // 2
    frequency = rope_base ** (-jnp.arange(half_width, dtype=jnp.float32) * 2.0 / width)
    angles = positions.astype(jnp.float32)[..., None] * frequency
    cosine_table = jnp.cos(angles)
    sine_table = jnp.sin(angles)
    return (
        jnp.concatenate([cosine_table, cosine_table], -1),
        jnp.concatenate([sine_table, sine_table], -1),
    )


def rotate(vector, cosine_table, sine_table):
    half_width = vector.shape[-1] // 2
    turned = jnp.concatenate([-vector[..., half_width:], vector[..., :half_width]], -1)
    return vector * cosine_table + turned * sine_table


def rotate_back(gradient, cosine_table, sine_table):
    half_width = gradient.shape[-1] // 2
    scaled = gradient * sine_table
    turned = jnp.concatenate([scaled[..., half_width:], -scaled[..., :half_width]], -1)
    return gradient * cosine_table + turned


def scale_of(vector):
    return lax.rsqrt(jnp.mean(vector * vector, axis=-1, keepdims=True) + epsilon)


def norm_back(gradient, normed, inverse, gain_vector):
    shaped = gradient * gain_vector
    vector_grad = inverse * (shaped - normed * jnp.mean(shaped * normed, axis=-1, keepdims=True))
    gain_grad = jnp.sum((gradient * normed).reshape(-1, gradient.shape[-1]), axis=0)
    return (vector_grad, gain_grad)


def score_block(query_seq, key_seq, segment_row):
    seq_length, key_heads, head_dim = key_seq.shape
    grouped = query_seq.reshape(seq_length, key_heads, -1, head_dim)
    scores = jnp.einsum(
        "ikgd,jkd->kgij", grouped, key_seq, preferred_element_type=jnp.float32
    ) * head_dim ** (-0.5)
    token_index = jnp.arange(seq_length)
    allowed = (segment_row[:, None] == segment_row[None, :]) & (
        token_index[None, :] <= token_index[:, None]
    )
    return (jnp.where(allowed, scores, -1000000000.0), grouped)


def attend_forward(members):
    query_seq, key_seq, value_seq, segment_row = members
    scores, grouped = score_block(query_seq, key_seq, segment_row)
    row_max = jnp.max(scores, -1, keepdims=True)
    exponent = jnp.exp(scores - row_max)
    row_total = jnp.sum(exponent, -1, keepdims=True)
    soft_probs = (exponent / row_total).astype(jnp.bfloat16)
    output = jnp.einsum("kgij,jkd->ikgd", soft_probs, value_seq, preferred_element_type=jnp.float32)
    return (
        output.reshape(query_seq.shape[0], -1).astype(jnp.bfloat16),
        row_max + jnp.log(row_total),
    )


def attend_backward(members):
    query_seq, key_seq, value_seq, segment_row, log_total, grad_seq = members
    seq_length, key_heads, head_dim = key_seq.shape
    scores, grouped = score_block(query_seq, key_seq, segment_row)
    soft_probs = jnp.exp(scores - log_total)
    grad_split = grad_seq.reshape(seq_length, key_heads, -1, head_dim)
    grad_probs = jnp.einsum(
        "ikgd,jkd->kgij", grad_split, value_seq, preferred_element_type=jnp.float32
    )
    value_part = jnp.einsum(
        "kgij,ikgd->jkd",
        soft_probs.astype(jnp.bfloat16),
        grad_split,
        preferred_element_type=jnp.float32,
    )
    row_delta = jnp.sum(grad_probs * soft_probs, -1, keepdims=True)
    score_grad = (soft_probs * (grad_probs - row_delta)).astype(jnp.bfloat16)
    score_scale = head_dim ** (-0.5)
    query_part = (
        jnp.einsum("kgij,jkd->ikgd", score_grad, key_seq, preferred_element_type=jnp.float32)
        * score_scale
    )
    key_part = (
        jnp.einsum("kgij,ikgd->jkd", score_grad, grouped, preferred_element_type=jnp.float32)
        * score_scale
    )
    return (
        query_part.reshape(seq_length, -1, head_dim).astype(jnp.bfloat16),
        key_part.astype(jnp.bfloat16),
        value_part.astype(jnp.bfloat16),
    )


def local(
    tokens,
    segments,
    attn_gain,
    mlp_gain,
    query_gain,
    key_gain,
    query_weight,
    key_matrix,
    value_matrix,
    output_weight,
    gate_weight,
    up_weight,
    down_weight,
    cotangent,
):
    gathered = (
        lax.all_gather(query_weight, "fsdp", axis=0, tiled=True),
        lax.all_gather(key_matrix, "fsdp", axis=0, tiled=True),
        lax.all_gather(value_matrix, "fsdp", axis=0, tiled=True),
        lax.all_gather(output_weight, "fsdp", axis=1, tiled=True),
        lax.all_gather(gate_weight, "fsdp", axis=0, tiled=True),
        lax.all_gather(up_weight, "fsdp", axis=0, tiled=True),
        lax.all_gather(down_weight, "fsdp", axis=1, tiled=True),
        lax.all_gather(attn_gain, "fsdp", axis=0, tiled=True),
        lax.all_gather(mlp_gain, "fsdp", axis=0, tiled=True),
        lax.all_gather(query_gain, "fsdp", axis=0, tiled=True),
        lax.all_gather(key_gain, "fsdp", axis=0, tiled=True),
    )
    (
        complete_query,
        complete_key,
        complete_value,
        complete_output,
        complete_gate,
        complete_up,
        complete_down,
    ) = gathered[:7]
    gain_attn, gain_mlp, gain_query, gain_key = [
        member.astype(jnp.float32) for member in gathered[7:]
    ]

    def rows_all(member):
        return lax.all_gather(member, "tensor", axis=1, tiled=True)

    def rows_sum(member):
        return lax.psum_scatter(member, "tensor", scatter_dimension=1, tiled=True)

    seq_count, local_rows, width = tokens.shape
    seq_length = segments.shape[1]
    head_dim = gain_query.shape[0]
    source = tokens.astype(jnp.float32)
    inverse_one = scale_of(source)
    normed_one = source * inverse_one
    first_hidden = rows_all((normed_one * gain_attn).astype(jnp.bfloat16))
    query_raw = jnp.einsum(
        "fta,ay->fty", first_hidden, complete_query, preferred_element_type=jnp.float32
    )
    unrotated_key = jnp.einsum(
        "fta,ay->fty", first_hidden, complete_key, preferred_element_type=jnp.float32
    )
    value_rows = jnp.einsum(
        "fta,ay->fty", first_hidden, complete_value, preferred_element_type=jnp.float32
    ).astype(jnp.bfloat16)
    cosine_table, sine_table = rope_tables(positions_of(segments), head_dim)
    cosine_table = cosine_table[:, :, None, :]
    sine_table = sine_table[:, :, None, :]
    query_split = query_raw.reshape(seq_count, seq_length, -1, head_dim)
    query_inverse = scale_of(query_split)
    query_normed = query_split * query_inverse
    query_rot = rotate(query_normed * gain_query, cosine_table, sine_table).astype(jnp.bfloat16)
    key_split = unrotated_key.reshape(seq_count, seq_length, -1, head_dim)
    key_inverse = scale_of(key_split)
    key_normed = key_split * key_inverse
    key_rot = rotate(key_normed * gain_key, cosine_table, sine_table).astype(jnp.bfloat16)
    value_split = value_rows.reshape(seq_count, seq_length, -1, head_dim)
    attended_rows, log_total = lax.map(attend_forward, (query_rot, key_rot, value_split, segments))
    attention_piece = jnp.einsum(
        "yig,gc->yic", attended_rows, complete_output, preferred_element_type=jnp.float32
    )
    middle = source + rows_sum(attention_piece)
    inverse_two = scale_of(middle)
    second_hidden = rows_all((middle * inverse_two * gain_mlp).astype(jnp.bfloat16))
    normed_two = middle * inverse_two
    gate_value = jnp.einsum(
        "fta,ay->fty", second_hidden, complete_gate, preferred_element_type=jnp.float32
    )
    up_projected = jnp.einsum(
        "fta,ay->fty", second_hidden, complete_up, preferred_element_type=jnp.float32
    )
    sigmoid_gate = jax.nn.sigmoid(gate_value)
    silu_gate = gate_value * sigmoid_gate
    active_product = (silu_gate * up_projected).astype(jnp.bfloat16)
    feedforward_piece = jnp.einsum(
        "yig,gc->yic", active_product, complete_down, preferred_element_type=jnp.float32
    )
    layer_out = (middle + rows_sum(feedforward_piece)).astype(jnp.bfloat16)
    grad_out = cotangent.astype(jnp.float32)
    feedforward_gradient = rows_all(cotangent)
    active_gradient = jnp.einsum(
        "fcp,jp->fcj", feedforward_gradient, complete_down, preferred_element_type=jnp.float32
    )
    down_piece = jnp.einsum(
        "hnk,hnj->kj", active_product, feedforward_gradient, preferred_element_type=jnp.float32
    )
    gate_row_values = (
        active_gradient * up_projected * (sigmoid_gate * (1.0 + gate_value * (1.0 - sigmoid_gate)))
    ).astype(jnp.bfloat16)
    up_row_values = (active_gradient * silu_gate).astype(jnp.bfloat16)
    gate_piece = jnp.einsum(
        "thu,thr->ur", second_hidden, gate_row_values, preferred_element_type=jnp.float32
    )
    up_piece = jnp.einsum(
        "thu,thr->ur", second_hidden, up_row_values, preferred_element_type=jnp.float32
    )
    hidden_two_part = jnp.einsum(
        "nvq,zq->nvz", gate_row_values, complete_gate, preferred_element_type=jnp.float32
    )
    hidden_two_part = hidden_two_part + jnp.einsum(
        "nvq,zq->nvz", up_row_values, complete_up, preferred_element_type=jnp.float32
    )
    back_two, mlp_gain_part = norm_back(
        rows_sum(hidden_two_part), normed_two, inverse_two, gain_mlp
    )
    grad_middle = grad_out + back_two
    attention_gradient = rows_all(grad_middle.astype(jnp.bfloat16))
    grad_mixed = jnp.einsum(
        "fcp,jp->fcj", attention_gradient, complete_output, preferred_element_type=jnp.float32
    ).astype(jnp.bfloat16)
    output_piece = jnp.einsum(
        "hnk,hnj->kj", attended_rows, attention_gradient, preferred_element_type=jnp.float32
    )
    query_back, key_back, value_back = lax.map(
        attend_backward, (query_rot, key_rot, value_split, segments, log_total, grad_mixed)
    )
    query_pre = rotate_back(query_back.astype(jnp.float32), cosine_table, sine_table)
    unrotated_query_gradient, query_gain_part = norm_back(
        query_pre, query_normed, query_inverse, gain_query
    )
    unrotated_query_gradient = unrotated_query_gradient.reshape(seq_count, seq_length, -1).astype(
        jnp.bfloat16
    )
    key_pre = rotate_back(key_back.astype(jnp.float32), cosine_table, sine_table)
    unrotated_key_gradient, key_gain_part = norm_back(key_pre, key_normed, key_inverse, gain_key)
    unrotated_key_gradient = unrotated_key_gradient.reshape(seq_count, seq_length, -1).astype(
        jnp.bfloat16
    )
    unrotated_value_gradient = value_back.reshape(seq_count, seq_length, -1)
    query_part = jnp.einsum(
        "thu,thr->ur", first_hidden, unrotated_query_gradient, preferred_element_type=jnp.float32
    )
    key_part = jnp.einsum(
        "thu,thr->ur", first_hidden, unrotated_key_gradient, preferred_element_type=jnp.float32
    )
    value_part = jnp.einsum(
        "thu,thr->ur", first_hidden, unrotated_value_gradient, preferred_element_type=jnp.float32
    )
    hidden_one_part = jnp.einsum(
        "nvq,zq->nvz", unrotated_query_gradient, complete_query, preferred_element_type=jnp.float32
    )
    hidden_one_part = hidden_one_part + jnp.einsum(
        "nvq,zq->nvz", unrotated_key_gradient, complete_key, preferred_element_type=jnp.float32
    )
    hidden_one_part = hidden_one_part + jnp.einsum(
        "nvq,zq->nvz", unrotated_value_gradient, complete_value, preferred_element_type=jnp.float32
    )
    back_one, attn_gain_part = norm_back(
        rows_sum(hidden_one_part), normed_one, inverse_one, gain_attn
    )
    grad_tokens = grad_middle + back_one
    gain_sums = lax.psum((attn_gain_part, mlp_gain_part, query_gain_part, key_gain_part), "tensor")
    grad_sums = (
        lax.psum_scatter(gain_sums[0], "fsdp", scatter_dimension=0, tiled=True),
        lax.psum_scatter(gain_sums[1], "fsdp", scatter_dimension=0, tiled=True),
        lax.psum_scatter(gain_sums[2], "fsdp", scatter_dimension=0, tiled=True),
        lax.psum_scatter(gain_sums[3], "fsdp", scatter_dimension=0, tiled=True),
        lax.psum_scatter(query_part, "fsdp", scatter_dimension=0, tiled=True),
        lax.psum_scatter(key_part, "fsdp", scatter_dimension=0, tiled=True),
        lax.psum_scatter(value_part, "fsdp", scatter_dimension=0, tiled=True),
        lax.psum_scatter(output_piece, "fsdp", scatter_dimension=1, tiled=True),
        lax.psum_scatter(gate_piece, "fsdp", scatter_dimension=0, tiled=True),
        lax.psum_scatter(up_piece, "fsdp", scatter_dimension=0, tiled=True),
        lax.psum_scatter(down_piece, "fsdp", scatter_dimension=1, tiled=True),
    )
    return (
        layer_out,
        grad_tokens,
        grad_sums[0],
        grad_sums[1],
        grad_sums[2],
        grad_sums[3],
        grad_sums[4],
        grad_sums[5],
        grad_sums[6],
        grad_sums[7],
        grad_sums[8],
        grad_sums[9],
        grad_sums[10],
    )


def solution(mesh):
    in_specs = (
        P("fsdp", "tensor", None),
        P("fsdp", None),
        P("fsdp"),
        P("fsdp"),
        P("fsdp"),
        P("fsdp"),
        P("fsdp", "tensor"),
        P("fsdp", "tensor"),
        P("fsdp", "tensor"),
        P("tensor", "fsdp"),
        P("fsdp", "tensor"),
        P("fsdp", "tensor"),
        P("tensor", "fsdp"),
        P("fsdp", "tensor", None),
    )
    out_specs = (
        P("fsdp", "tensor", None),
        P("fsdp", "tensor", None),
        P("fsdp"),
        P("fsdp"),
        P("fsdp"),
        P("fsdp"),
        P("fsdp", "tensor"),
        P("fsdp", "tensor"),
        P("fsdp", "tensor"),
        P("tensor", "fsdp"),
        P("fsdp", "tensor"),
        P("fsdp", "tensor"),
        P("tensor", "fsdp"),
    )
    return jax.shard_map(local, mesh=mesh, in_specs=in_specs, out_specs=out_specs, check_vma=False)
```

profile of v0, /device:TPU:0, one launch (start us, length us, event | category | flops | bytes accessed | tf_op | source)
XLA Modules:
  0.0 1398.0 jit_solution(3849900285777397274)
XLA Ops:
  14.0 35.8 %all-reduce.10 = (bf16[1024]{0:T(1024)(128)(2,1)S(1)}, bf16[128]{0:T(256)(128)(2,1)S(1)}, bf16[128]{0:T(256)(128)(2,1)S(1)}, bf16[1024]{0:T(1024)(128)(2,1)S(1)}) all-reduce(bf16[1024]{0:T(1024)(128)(2,1)S(1)} %dynamic-update-slice, bf16[128]{0:T(256)(128)(2,1)S(1)} %dynamic-update-slice.1, ...), channel_id=1, replica_groups=mesh['fsdp'=16,'tensor'=2] {'fsdp'}, use_global_device_ids=true, to_apply=%add | all-reduce | flops 2304 | bytes 9216
  59.1 26.1 %all-gather.12.cloned.1.call-done = bf16[1,1024,1024]{2,1,0:T(8,128)(2,1)} async-done(((bf16[1,512,1024]{2,1,0:T(8,128)(2,1)}), bf16[1,1024,1024]{2,1,0:T(8,128)(2,1)}) %all-gather.12.cloned.1.call-update) | async-done | bytes 2097168 | tf_op jit(solution)/shard_map/all_gather | solution.py:163
  91.5 34.0 %all-gather.14.cloned.1.call-done = bf16[1024,512]{1,0:T(8,128)(2,1)} async-done(((bf16[64,512]{1,0:T(8,128)(2,1)}), bf16[1024,512]{1,0:T(8,128)(2,1)}) %all-gather.14.cloned.1.call-update) | async-done | bytes 1048592 | tf_op jit(solution)/shard_map/all_gather | solution.py:139
  129.6 38.2 %all-gather.18.cloned.1.call-done = bf16[1024,1024]{1,0:T(8,128)(2,1)} async-done(((bf16[64,1024]{1,0:T(8,128)(2,1)}), bf16[1024,1024]{1,0:T(8,128)(2,1)}) %all-gather.18.cloned.1.call-update) | async-done | bytes 2097168 | tf_op jit(solution)/shard_map/all_gather | solution.py:137
  181.1 14.7 %fusion.9 = (f32[4,2,1024]{2,1,0:T(2,128)S(1)}, f32[4,1024,1024,2]{2,1,3,0:T(8,128)}) fusion(pred[1024,1024]{0,1:T(8,128)(4,1)S(1)} %fusion.18, bf16[1024,4,128,1]{0,2,3,1:T(8,128)(2,1)S(1)} %copy-done.16, bf16[1024,4,2,128]{0,3,2,1:T(8,128)(2,1)S(1)} %fusion.15), kind=kOutput, calls=%fused_computation.14 | convolution fusion | flops 2172641280 | bytes 37781504 | tf_op jit(solution)/shard_map/while/body/eval_jaxpr/ikgd,jkd->kgij/dot_general | solution.py:63
  195.8 14.4 %fusion.3 = f32[4,2,1024]{2,1,0:T(2,128)S(1)} fusion(f32[4,2,1024]{2,1,0:T(2,128)S(1)} %get-tuple-element.103, f32[4,1024,1024,2]{2,1,3,0:T(8,128)} %get-tuple-element.104, pred[1024,1024]{0,1:T(8,128)(4,1)S(1)} %fusion.18), kind=kLoop, calls=%fused_computation.9 | loop fusion | flops 33546240 | bytes 34668544 | tf_op jit(solution)/shard_map/while/body/eval_jaxpr/reduce_sum | solution.py:78
  210.3 15.2 %fusion.63 = bf16[4,128,2,1024]{3,1,2,0:T(8,128)(2,1)S(1)} fusion(bf16[1024,4,128,1]{0,2,3,1:T(8,128)(2,1)S(1)} %bitcast.259, f32[4,2,1024]{2,1,0:T(2,128)S(1)} %fusion.3, f32[4,2,1024]{2,1,0:T(2,128)S(1)} %get-tuple-element.103, f32[4,1024,1024,2]{2,1,3,0:T(8,128)} %get-tuple-element.104, pred[1024,1024]{0,1:T(8,128)(4,1)S(1)} %fusion.18), kind=kOutput, calls=%fused_computation.112 | convolution fusion | flops 2190475264 | bytes 37814272 | tf_op jit(solution)/shard_map/while/body/eval_jaxpr/kgij,jkd->ikgd/dot_general | solution.py:80
  233.2 52.4 %reduce-scatter.12.cloned.1.call-done = f32[1,512,1024]{2,1,0:T(8,128)} async-done(((f32[1,1024,1024]{2,1,0:T(8,128)}), f32[1,512,1024]{2,1,0:T(8,128)}) %reduce-scatter.12.cloned.1.call-update) | async-done | bytes 2097168 | tf_op jit(solution)/shard_map/reduce_scatter | solution.py:166
  291.6 41.8 %all-gather.26.cloned.1.call-done = bf16[1024,1536]{1,0:T(8,128)(2,1)} async-done(((bf16[64,1536]{1,0:T(8,128)(2,1)}), bf16[1024,1536]{1,0:T(8,128)(2,1)}) %all-gather.26.cloned.1.call-update) | async-done | bytes 3145744 | tf_op jit(solution)/shard_map/all_gather | solution.py:142
  333.3 33.6 %all-gather.22.cloned.1.call-done = bf16[1,1024,1024]{2,1,0:T(8,128)(2,1)} async-done(((bf16[1,512,1024]{2,1,0:T(8,128)(2,1)}), bf16[1,1024,1024]{2,1,0:T(8,128)(2,1)}) %all-gather.22.cloned.1.call-update) | async-done | bytes 2097168 | tf_op jit(solution)/shard_map/all_gather | solution.py:163
  375.4 39.5 %all-gather.24.cloned.1.call-done = bf16[1024,1536]{1,0:T(8,128)(2,1)} async-done(((bf16[64,1536]{1,0:T(8,128)(2,1)}), bf16[1024,1536]{1,0:T(8,128)(2,1)}) %all-gather.24.cloned.1.call-update) | async-done | bytes 3145744 | tf_op jit(solution)/shard_map/all_gather | solution.py:141
  423.5 24.8 %all-gather.30.cloned.1.call-done = bf16[1,1024,1024]{2,1,0:T(8,128)(2,1)} async-done(((bf16[1,512,1024]{2,1,0:T(8,128)(2,1)}), bf16[1,1024,1024]{2,1,0:T(8,128)(2,1)}) %all-gather.30.cloned.1.call-update) | async-done | bytes 2097168 | tf_op jit(solution)/shard_map/all_gather | solution.py:163
  448.3 47.8 %all-gather.28.cloned.1.call-done = bf16[1536,1024]{0,1:T(8,128)(2,1)} async-done(((bf16[1536,64]{0,1:T(8,128)(2,1)}), bf16[1536,1024]{0,1:T(8,128)(2,1)}) %all-gather.28.cloned.1.call-update) | async-done | bytes 3145744 | tf_op jit(solution)/shard_map/all_gather | solution.py:143
  496.1 11.8 multiply_convert_fusion
  517.2 53.2 %reduce-scatter.16.cloned.1.call-done = f32[1,512,1024]{2,1,0:T(8,128)} async-done(((f32[1,1024,1024]{2,1,0:T(8,128)}), f32[1,512,1024]{2,1,0:T(8,128)}) %reduce-scatter.16.cloned.1.call-update) | async-done | bytes 2097168 | tf_op jit(solution)/shard_map/reduce_scatter | solution.py:166
  575.3 33.0 %all-gather.32.cloned.1.call-done = bf16[1,1024,1024]{2,1,0:T(8,128)(2,1)} async-done(((bf16[1,512,1024]{2,1,0:T(8,128)(2,1)}), bf16[1,1024,1024]{2,1,0:T(8,128)(2,1)}) %all-gather.32.cloned.1.call-update) | async-done | bytes 2097168 | tf_op jit(solution)/shard_map/all_gather | solution.py:163
  612.9 16.3 %bitcast_convert_fusion = bf16[4,128,1024]{2,1,0:T(8,128)(2,1)} fusion(bf16[1024,4,2,128]{0,3,2,1:T(8,128)(2,1)S(1)} %bitcast.256, f32[4,2,1024]{2,1,0:T(2,128)S(1)} %bitcast.264, f32[4,1024,1024,2]{2,1,3,0:T(8,128)} %get-tuple-element.104, pred[1024,1024]{0,1:T(8,128)(4,1)S(1)} %fusion.18), kind=kOutput, calls=%fused_computation.67 | convolution fusion | flops 2181562368 | bytes 37781504 | tf_op jit(solution)/shard_map/while/body/eval_jaxpr/kgij,ikgd->jkd/dot_general | solution.py:96
  629.2 24.6 %fusion = (f32[4,2,1024]{2,1,0:T(2,128)S(1)}, f32[4,1024,1024,2]{2,1,3,0:T(8,128)}) fusion(f32[4,2,1024]{2,1,0:T(2,128)S(1)} %bitcast.265, f32[4,1024,1024,2]{2,1,3,0:T(8,128)} %get-tuple-element.104, pred[1024,1024]{0,1:T(8,128)(4,1)S(1)} %fusion.18, bf16[1024,4,128,1]{0,2,3,1:T(8,128)(2,1)} %bitcast.258, bf16[1024,4,2,128]{0,3,2,1:T(8,128)(2,1)S(1)} %bitcast.257), kind=kOutput, calls=%fused_computation.2 | convolution fusion | flops 2189418496 | bytes 71368704 | tf_op jit(solution)/shard_map/while/body/eval_jaxpr/ikgd,jkd->kgij/dot_general | solution.py:93
  653.7 28.6 %fusion.2 = bf16[4,2,1024,1024]{2,3,1,0:T(8,128)(2,1)} fusion(f32[4,1024,1024,2]{2,1,3,0:T(8,128)} %get-tuple-element.106, f32[4,2,1024]{2,1,0:T(2,128)S(1)} %get-tuple-element.105, f32[4,2,1024]{2,1,0:T(2,128)S(1)} %bitcast.266, f32[4,1024,1024,2]{2,1,3,0:T(8,128)} %get-tuple-element.104, pred[1024,1024]{0,1:T(8,128)(4,1)S(1)} %fusion.18), kind=kLoop, calls=%fused_computation.4 | loop fusion | flops 50331648 | bytes 85000192 | tf_op jit(solution)/shard_map/while/body/eval_jaxpr/convert_element_type | solution.py:103
  682.3 12.2 fusion.34
  737.5 8.6 fusion.39
  746.4 8.6 fusion.43
  755.1 8.8 fusion.45
  790.0 34.1 %all-reduce.8 = (f32[1024]{0:T(1024)S(1)}, f32[1024]{0:T(1024)S(1)}, f32[128]{0:T(128)S(1)}, f32[128]{0:T(128)S(1)}) all-reduce(f32[1024]{0:T(1024)S(1)} %get-tuple-element.70, f32[1024]{0:T(1024)S(1)} %copy-done.39, f32[128]{0:T(128)S(1)} %get-tuple-element.54, ...), channel_id=6, replica_groups=mesh['fsdp'=16,'tensor'=2] {'fsdp'}, use_global_device_ids=true, to_apply=%region_19.20.clone | all-reduce | flops 2304 | bytes 18432
  829.9 10.4 reduce-scatter.14.cloned.1.call-done
  845.1 84.8 %reduce-scatter.32.cloned.1.call-done = f32[1536,64]{0,1:T(8,128)} async-done(((f32[1536,1024]{0,1:T(8,128)}), f32[1536,64]{0,1:T(8,128)}) %reduce-scatter.32.cloned.1.call-update) | async-done | bytes 393232 | tf_op jit(solution)/shard_map/reduce_scatter | solution.py:302
  929.9 89.4 %reduce-scatter.30.cloned.1.call-done = f32[64,1536]{1,0:T(8,128)} async-done(((f32[1024,1536]{1,0:T(8,128)}), f32[64,1536]{1,0:T(8,128)}) %reduce-scatter.30.cloned.1.call-update) | async-done | bytes 393232 | tf_op jit(solution)/shard_map/reduce_scatter | solution.py:301
  1019.3 88.9 %reduce-scatter.28.cloned.1.call-done = f32[64,1536]{1,0:T(8,128)} async-done(((f32[1024,1536]{1,0:T(8,128)}), f32[64,1536]{1,0:T(8,128)}) %reduce-scatter.28.cloned.1.call-update) | async-done | bytes 393232 | tf_op jit(solution)/shard_map/reduce_scatter | solution.py:300
  1108.2 65.5 %reduce-scatter.24.cloned.1.call-done = f32[64,512]{1,0:T(8,128)} async-done(((f32[1024,512]{1,0:T(8,128)}), f32[64,512]{1,0:T(8,128)}) %reduce-scatter.24.cloned.1.call-update) | async-done | bytes 131088 | tf_op jit(solution)/shard_map/reduce_scatter | solution.py:298
  1173.7 64.7 %reduce-scatter.22.cloned.1.call-done = f32[64,512]{1,0:T(8,128)} async-done(((f32[1024,512]{1,0:T(8,128)}), f32[64,512]{1,0:T(8,128)}) %reduce-scatter.22.cloned.1.call-update) | async-done | bytes 131088 | tf_op jit(solution)/shard_map/reduce_scatter | solution.py:297
  1238.5 76.3 %reduce-scatter.26.cloned.1.call-done = f32[1024,64]{0,1:T(8,128)} async-done(((f32[1024,1024]{0,1:T(8,128)}), f32[1024,64]{0,1:T(8,128)}) %reduce-scatter.26.cloned.1.call-update) | async-done | bytes 262160 | tf_op jit(solution)/shard_map/reduce_scatter | solution.py:299
  1314.7 76.0 %reduce-scatter.20.cloned.1.call-done = f32[64,1024]{1,0:T(8,128)} async-done(((f32[1024,1024]{1,0:T(8,128)}), f32[64,1024]{1,0:T(8,128)}) %reduce-scatter.20.cloned.1.call-update) | async-done | bytes 262160 | tf_op jit(solution)/shard_map/reduce_scatter | solution.py:296
  (231 shorter events, 165.7 us)
Async XLA Ops:
  7.2 52.0 %all-gather.16.cloned.1.call-start = ((), (), s32[]{:S(2)}) async-start(), calls=%async_computation.13 | async-start | bytes 1114112 | tf_op jit(solution)/shard_map/all_gather | solution.py:138
  7.9 77.4 %all-gather.12.cloned.1.call-start = ((), (), s32[]{:S(2)}) async-start(), calls=%async_computation.11 | async-start | bytes 3145728 | tf_op jit(solution)/shard_map/all_gather | solution.py:163
  54.4 71.0 %all-gather.14.cloned.1.call-start = ((), (), s32[]{:S(2)}) async-start(), calls=%async_computation.12 | async-start | bytes 1114112 | tf_op jit(solution)/shard_map/all_gather | solution.py:139
  55.2 112.6 %all-gather.18.cloned.1.call-start = ((), (), s32[]{:S(2)}) async-start(), calls=%async_computation.14 | async-start | bytes 2228224 | tf_op jit(solution)/shard_map/all_gather | solution.py:137
  55.8 169.8 %all-gather.20.cloned.1.call-start = ((), (), s32[]{:S(2)}) async-start(), calls=%async_computation.15 | async-start | bytes 2228224 | tf_op jit(solution)/shard_map/all_gather | solution.py:140
  56.3 229.2 %reduce-scatter.12.cloned.1.call-start = ((), (), s32[]{:S(2)}) async-start(), calls=%async_computation.16 | async-start | bytes 6291456 | tf_op jit(solution)/shard_map/reduce_scatter | solution.py:166
  56.4 33.0 %copy-start.40 = (f32[128]{0:T(128)}, f32[128]{0:T(128)S(1)}, u32[]{:S(2)}) copy-start(f32[128]{0:T(128)S(1)} %convert_element_type.195) | copy-start | bytes 1540
  59.1 118.8 %copy-start.9 = (f32[1024,128]{0,1:T(8,128)}, f32[1024,128]{0,1:T(8,128)S(1)}, u32[]{:S(2)}) copy-start(f32[1024,128]{0,1:T(8,128)S(1)} %get-tuple-element.107) | copy-start | bytes 1572868
  59.1 118.8 %copy-start.12 = (f32[1024,128]{0,1:T(8,128)}, f32[1024,128]{0,1:T(8,128)S(1)}, u32[]{:S(2)}) copy-start(f32[1024,128]{0,1:T(8,128)S(1)} %get-tuple-element.108) | copy-start | bytes 1572868
  232.3 101.0 %all-gather.26.cloned.1.call-start = ((), (), s32[]{:S(2)}) async-start(), calls=%async_computation.19 | async-start | bytes 3342336 | tf_op jit(solution)/shard_map/all_gather | solution.py:142
  233.1 133.8 %all-gather.22.cloned.1.call-start = ((), (), s32[]{:S(2)}) async-start(), calls=%async_computation.17 | async-start | bytes 3145728 | tf_op jit(solution)/shard_map/all_gather | solution.py:163
  233.1 340.2 %copy-start.28 = (f32[1024]{0:T(1024)}, f32[1024]{0:T(1024)S(1)}, u32[]{:S(2)}) copy-start(f32[1024]{0:T(1024)S(1)} %convert_element_type.204) | copy-start | bytes 12292
  287.7 285.6 %copy-start.6 = (f32[1,512,1024]{2,1,0:T(8,128)}, f32[1,512,1024]{2,1,0:T(8,128)S(1)}, u32[]{:S(2)}) copy-start(f32[1,512,1024]{2,1,0:T(8,128)S(1)} %get-tuple-element.85) | copy-start | bytes 6291460
  287.8 285.6 %copy-start.33 = (f32[512]{0:T(512)}, f32[512]{0:T(512)S(1)}, u32[]{:S(2)}) copy-start(f32[512]{0:T(512)S(1)} %add_rsqrt_fusion.2) | copy-start | bytes 6148
  289.3 125.6 %all-gather.24.cloned.1.call-start = ((), (), s32[]{:S(2)}) async-start(), calls=%async_computation.18 | async-start | bytes 3342336 | tf_op jit(solution)/shard_map/all_gather | solution.py:141
  290.0 158.3 %all-gather.30.cloned.1.call-start = ((), (), s32[]{:S(2)}) async-start(), calls=%async_computation.22 | async-start | bytes 3145728 | tf_op jit(solution)/shard_map/all_gather | solution.py:163
  290.6 205.5 %all-gather.28.cloned.1.call-start = ((), (), s32[]{:S(2)}) async-start(), calls=%async_computation.20 | async-start | bytes 3342336 | tf_op jit(solution)/shard_map/all_gather | solution.py:143
  291.3 279.1 %reduce-scatter.16.cloned.1.call-start = ((), (), s32[]{:S(2)}) async-start(), calls=%async_computation.23 | async-start | bytes 6291456 | tf_op jit(solution)/shard_map/reduce_scatter | solution.py:166
  517.2 91.1 %all-gather.32.cloned.1.call-start = ((), (), s32[]{:S(2)}) async-start(), calls=%async_computation.24 | async-start | bytes 3145728 | tf_op jit(solution)/shard_map/all_gather | solution.py:163
  575.0 212.7 %reduce-scatter.18.cloned.1.call-start = ((), (), s32[]{:S(2)}) async-start(), calls=%async_computation.25 | async-start | bytes 6291456 | tf_op jit(solution)/shard_map/reduce_scatter | solution.py:166
  729.1 111.1 %reduce-scatter.14.cloned.1.call-start = ((), (), s32[]{:S(2)}) async-start(), calls=%async_computation.21 | async-start | bytes 6291456 | tf_op jit(solution)/shard_map/reduce_scatter | solution.py:166
  737.5 192.4 %reduce-scatter.32.cloned.1.call-start = ((), (), s32[]{:S(2)}) async-start(), calls=%async_computation.32 | async-start | bytes 6684672 | tf_op jit(solution)/shard_map/reduce_scatter | solution.py:302
  746.2 273.1 %reduce-scatter.30.cloned.1.call-start = ((), (), s32[]{:S(2)}) async-start(), calls=%async_computation.31 | async-start | bytes 6684672 | tf_op jit(solution)/shard_map/reduce_scatter | solution.py:301
  755.1 353.1 %reduce-scatter.28.cloned.1.call-start = ((), (), s32[]{:S(2)}) async-start(), calls=%async_computation.30 | async-start | bytes 6684672 | tf_op jit(solution)/shard_map/reduce_scatter | solution.py:300
  763.9 409.8 %reduce-scatter.24.cloned.1.call-start = ((), (), s32[]{:S(2)}) async-start(), calls=%async_computation.28 | async-start | bytes 2228224 | tf_op jit(solution)/shard_map/reduce_scatter | solution.py:298
  768.5 470.0 %reduce-scatter.22.cloned.1.call-start = ((), (), s32[]{:S(2)}) async-start(), calls=%async_computation.27 | async-start | bytes 2228224 | tf_op jit(solution)/shard_map/reduce_scatter | solution.py:297
  773.1 541.7 %reduce-scatter.26.cloned.1.call-start = ((), (), s32[]{:S(2)}) async-start(), calls=%async_computation.29 | async-start | bytes 4456448 | tf_op jit(solution)/shard_map/reduce_scatter | solution.py:299
  779.8 610.9 %reduce-scatter.20.cloned.1.call-start = ((), (), s32[]{:S(2)}) async-start(), calls=%async_computation.26 | async-start | bytes 4456448 | tf_op jit(solution)/shard_map/reduce_scatter | solution.py:296
  786.1 54.1 %copy-start.7 = (f32[1,512,1024]{2,1,0:T(8,128)S(1)}, f32[1,512,1024]{2,1,0:T(8,128)}, u32[]{:S(2)}) copy-start(f32[1,512,1024]{2,1,0:T(8,128)} %copy-done.6) | copy-start | bytes 6291460
  786.1 54.1 %copy-start.29 = (f32[1024]{0:T(1024)S(1)}, f32[1024]{0:T(1024)}, u32[]{:S(2)}) copy-start(f32[1024]{0:T(1024)} %copy-done.28) | copy-start | bytes 12292
  786.1 54.1 %copy-start.34 = (f32[512]{0:T(512)S(1)}, f32[512]{0:T(512)}, u32[]{:S(2)}) copy-start(f32[512]{0:T(512)} %copy-done.33) | copy-start | bytes 6148
  786.1 54.1 %copy-start.38 = (f32[512]{0:T(512)S(1)}, f32[512]{0:T(512)}, u32[]{:S(2)}) copy-start(f32[512]{0:T(512)} %copy-done.37) | copy-start | bytes 6148
  (39 other events, 167.7 us)
Sparse Core Ops, SparseCore 0:
  10.2 40.7 all-gather.15
  54.6 30.6 all-gather.11
  87.5 37.9 all-gather.13
  127.4 40.3 all-gather.17
  169.8 40.1 all-gather.19
  232.5 53.0 reduce-scatter.11
  288.1 45.1 all-gather.25
  334.9 31.9 all-gather.21
  369.4 45.4 all-gather.23
  416.4 31.9 all-gather.29
  450.9 45.1 all-gather.27
  517.3 53.0 reduce-scatter.15
  575.1 33.1 all-gather.31
  729.2 54.2 reduce-scatter.17
  785.8 54.3 reduce-scatter.13
  844.6 85.2 reduce-scatter.31
  934.8 84.4 reduce-scatter.29
  1023.7 84.4 reduce-scatter.27
  1113.0 60.6 reduce-scatter.23
  1177.9 60.5 reduce-scatter.21
  1243.4 71.2 reduce-scatter.25
  1319.1 71.5 reduce-scatter.19
where the time goes:
time: 1410 us; the launch traced here: 1400 us
  waiting for transfers between devices  986 us (70%)
  matrix products  215 us (15%)
  other arithmetic  87.6 us (6%)
  blocking collectives  75.3 us (5%)
  between operations  18.5 us (1%)
  local copies, waits for them, and re-layouts  14.4 us (1%)
    all_gather x4, waiting for transfers between devices, rows_all(): return lax.all_gather(member, 'tensor', axis=1, tiled=True)  118 us
    reduce_scatter x4, waiting for transfers between devices, rows_sum(): return lax.psum_scatter(member, 'tensor', scatter_dimension=1, tiled=True)  116 us
    reduce_scatter x1, waiting for transfers between devices, local(): lax.psum_scatter(up_piece, 'fsdp', scatter_dimension=0, tiled=True)  89.4 us
    reduce_scatter x1, waiting for transfers between devices, local(): lax.psum_scatter(gate_piece, 'fsdp', scatter_dimension=0, tiled=True)  88.9 us
    reduce_scatter x1, waiting for transfers between devices, local(): lax.psum_scatter(down_piece, 'fsdp', scatter_dimension=1, tiled=True)  84.8 us
    reduce_scatter x1, waiting for transfers between devices, local(): lax.psum_scatter(output_piece, 'fsdp', scatter_dimension=1, tiled=True)  76.3 us
    reduce_scatter x1, waiting for transfers between devices, local(): lax.psum_scatter(query_part, 'fsdp', scatter_dimension=0, tiled=True)  76 us
    unnamed x2, blocking collectives  69.9 us
  transfers between devices with their start and end apart: 22, of which 19 were waited for; matrix products, arithmetic and copies ran while one was open for 11% of the time, Pallas kernels for 0%

commit v1 on v0

v1 whole, which is shorter than its diff:
```python
import functools

import jax
import jax.numpy as jnp
from jax import lax
from jax.experimental import pallas as pl
from jax.experimental.pallas import tpu as pltpu
from jax.sharding import PartitionSpec as P

epsilon = 1e-06
rope_base = 1000000.0
LANES = 128
BF = jnp.bfloat16
F32 = jnp.float32


def starts_of(segment_rows):
    seq_length = segment_rows.shape[-1]
    token_index = jnp.arange(seq_length, dtype=jnp.int32)
    change = jnp.concatenate(
        [
            jnp.ones(segment_rows.shape[:-1] + (1,), bool),
            segment_rows[..., 1:] != segment_rows[..., :-1],
        ],
        axis=-1,
    )
    return lax.cummax(jnp.where(change, token_index, 0), axis=segment_rows.ndim - 1)


def rope_tables(positions, width):
    half_width = width // 2
    frequency = rope_base ** (-jnp.arange(half_width, dtype=F32) * 2.0 / width)
    angles = positions.astype(F32)[..., None] * frequency
    cosine_table = jnp.cos(angles)
    sine_table = jnp.sin(angles)
    return (
        jnp.concatenate([cosine_table, cosine_table], -1),
        jnp.concatenate([-sine_table, sine_table], -1),
    )


def scale_of(vector):
    return lax.rsqrt(jnp.mean(vector * vector, axis=-1, keepdims=True) + epsilon)


def nt(left, right):
    return lax.dot_general(left, right, (((1,), (1,)), ((), ())), preferred_element_type=F32)


def nn(left, right):
    return jnp.dot(left, right, preferred_element_type=F32)


def tn(left, right):
    return lax.dot_general(left, right, (((0,), (0,)), ((), ())), preferred_element_type=F32)


def turn(vector):
    return pltpu.roll(vector, vector.shape[1] // 2, 1)


def prepared(raw, gain, cosine, sine):
    inverse = scale_of(raw)
    normed = raw * inverse
    gained = normed * gain
    return (gained * cosine + turn(gained) * sine).astype(BF), normed, inverse


def scores_block(key_part, query_part, starts, first_row, scale):
    scores = nt(key_part, query_part) * scale
    key_index = lax.broadcasted_iota(jnp.int32, scores.shape, 0)
    query_index = lax.broadcasted_iota(jnp.int32, scores.shape, 1) + first_row
    allowed = (key_index <= query_index) & (key_index >= starts)
    return jnp.where(allowed, scores, -1000000000.0)


def soft_block(scores):
    exponent = jnp.exp(scores - jnp.max(scores, axis=0, keepdims=True))
    return exponent * (1.0 / jnp.sum(exponent, axis=0, keepdims=True))


def forward_kernel(
    group, block, q_ref, k_ref, v_ref, cos_ref, sin_ref, starts_ref, qg_ref, kg_ref, out_ref
):
    seq_length, head_dim = k_ref.shape
    scale = head_dim**-0.5
    cosine, sine = cos_ref[...], sin_ref[...]
    key_rot, _, _ = prepared(k_ref[...], kg_ref[...], cosine, sine)
    value_turned = v_ref[...].T.astype(BF)
    for head in range(group):
        columns = slice(head * head_dim, (head + 1) * head_dim)
        query_rot, _, _ = prepared(q_ref[:, columns], qg_ref[...], cosine, sine)
        for first in range(0, seq_length, block):
            last = first + block
            scores = scores_block(
                key_rot[:last], query_rot[first:last], starts_ref[:, first:last], first, scale
            )
            probs = soft_block(scores).astype(BF)
            out_ref[first:last, columns] = nn(value_turned[:, :last], probs).T.astype(BF)


def backward_kernel(
    group,
    block,
    q_ref,
    k_ref,
    v_ref,
    grad_ref,
    cos_ref,
    sin_ref,
    starts_ref,
    qg_ref,
    kg_ref,
    dq_ref,
    dk_ref,
    dv_ref,
    gains_ref,
    key_total,
    value_total,
    query_total,
):
    seq_length, head_dim = k_ref.shape
    scale = head_dim**-0.5
    cosine, sine = cos_ref[...], sin_ref[...]
    key_gain, query_gain = kg_ref[...], qg_ref[...]
    key_rot, key_normed, key_inverse = prepared(k_ref[...], key_gain, cosine, sine)
    key_turned = key_rot.astype(F32).T.astype(BF)
    value = v_ref[...].astype(BF)

    def norm_back(rounded, normed, inverse, gain):
        gradient = rounded.astype(BF).astype(F32)
        gradient = gradient * cosine - turn(gradient) * sine
        gain_grad = jnp.sum(gradient * normed, axis=0, keepdims=True)
        shaped = gradient * gain
        inner = jnp.mean(shaped * normed, axis=-1, keepdims=True)
        return (inverse * (shaped - normed * inner)).astype(BF), gain_grad

    key_total[...] = jnp.zeros_like(key_total)
    value_total[...] = jnp.zeros_like(value_total)
    gain_total = jnp.zeros((1, head_dim), F32)
    for head in range(group):
        columns = slice(head * head_dim, (head + 1) * head_dim)
        query_rot, query_normed, query_inverse = prepared(
            q_ref[:, columns], query_gain, cosine, sine
        )
        for first in range(0, seq_length, block):
            last = first + block
            query_part = query_rot[first:last]
            grad_part = grad_ref[first:last, columns]
            probs = soft_block(
                scores_block(key_rot[:last], query_part, starts_ref[:, first:last], first, scale)
            )
            grad_probs = nt(value[:last], grad_part)
            delta = jnp.sum(grad_probs * probs, axis=0, keepdims=True)
            score_grad = (probs * (grad_probs - delta)).astype(BF)
            value_total[:last, :] += nn(probs.astype(BF), grad_part)
            key_total[:last, :] += nn(score_grad, query_part)
            query_total[first:last, :] = nn(key_turned[:, :last], score_grad).T
        query_back, gain_part = norm_back(
            query_total[...] * scale, query_normed, query_inverse, query_gain
        )
        dq_ref[:, columns] = query_back
        gain_total = gain_total + gain_part
    key_back, key_gain_part = norm_back(key_total[...] * scale, key_normed, key_inverse, key_gain)
    dk_ref[...] = key_back
    dv_ref[...] = value_total[...].astype(BF)
    gains_ref[0:1, :] = gain_total
    gains_ref[1:2, :] = key_gain_part


def attention_specs(seq_length, query_width, key_width, head_dim):
    key_heads = key_width // head_dim
    group = query_width // key_width
    key_base = query_width // head_dim
    value_base = key_base + key_heads
    raw = [
        pl.BlockSpec((seq_length, group * head_dim), lambda s, h: (s, h)),
        pl.BlockSpec((seq_length, head_dim), lambda s, h: (s, key_base + h)),
        pl.BlockSpec((seq_length, head_dim), lambda s, h: (s, value_base + h)),
    ]
    tables = [
        pl.BlockSpec((seq_length, head_dim), lambda s, h: (s, 0)),
        pl.BlockSpec((seq_length, head_dim), lambda s, h: (s, 0)),
        pl.BlockSpec((None, 1, seq_length), lambda s, h: (s, 0, 0)),
        pl.BlockSpec((1, head_dim), lambda s, h: (0, 0)),
        pl.BlockSpec((1, head_dim), lambda s, h: (0, 0)),
    ]
    return raw, tables, group, key_heads


def attend_forward(qkv, tables, seq_count, query_width, key_width):
    seq_length = qkv.shape[0] // seq_count
    head_dim = tables[0].shape[-1]
    raw_specs, table_specs, group, key_heads = attention_specs(
        seq_length, query_width, key_width, head_dim
    )
    block = min(256, seq_length)
    return pl.pallas_call(
        functools.partial(forward_kernel, group, block),
        grid=(seq_count, key_heads),
        in_specs=raw_specs + table_specs,
        out_specs=pl.BlockSpec((seq_length, group * head_dim), lambda s, h: (s, h)),
        out_shape=jax.ShapeDtypeStruct((qkv.shape[0], query_width), BF),
        compiler_params=pltpu.CompilerParams(vmem_limit_bytes=40 * 2**20),
        cost_estimate=pl.CostEstimate(
            flops=3 * seq_count * seq_length * seq_length * query_width,
            bytes_accessed=qkv.size * 4 + qkv.shape[0] * query_width * 2,
            transcendentals=seq_count * seq_length * seq_length * query_width // head_dim,
        ),
    )(qkv, qkv, qkv, *tables)


def attend_backward(qkv, grad_mixed, tables, seq_count, query_width, key_width):
    seq_length = qkv.shape[0] // seq_count
    head_dim = tables[0].shape[-1]
    raw_specs, table_specs, group, key_heads = attention_specs(
        seq_length, query_width, key_width, head_dim
    )
    block = min(256, seq_length)
    rows = qkv.shape[0]
    wide = pl.BlockSpec((seq_length, group * head_dim), lambda s, h: (s, h))
    narrow = pl.BlockSpec((seq_length, head_dim), lambda s, h: (s, h))
    return pl.pallas_call(
        functools.partial(backward_kernel, group, block),
        grid=(seq_count, key_heads),
        in_specs=raw_specs + [wide] + table_specs,
        out_specs=[
            wide,
            narrow,
            narrow,
            pl.BlockSpec((None, None, 2, head_dim), lambda s, h: (s, h, 0, 0)),
        ],
        out_shape=[
            jax.ShapeDtypeStruct((rows, query_width), BF),
            jax.ShapeDtypeStruct((rows, key_width), BF),
            jax.ShapeDtypeStruct((rows, key_width), BF),
            jax.ShapeDtypeStruct((seq_count, key_heads, 2, head_dim), F32),
        ],
        scratch_shapes=[pltpu.VMEM((seq_length, head_dim), F32)] * 3,
        compiler_params=pltpu.CompilerParams(vmem_limit_bytes=48 * 2**20),
        cost_estimate=pl.CostEstimate(
            flops=7 * seq_count * seq_length * seq_length * query_width,
            bytes_accessed=qkv.size * 6 + rows * query_width * 2,
            transcendentals=seq_count * seq_length * seq_length * query_width // head_dim,
        ),
    )(qkv, qkv, qkv, grad_mixed, *tables)


def local(
    n_tensor,
    tokens,
    segments,
    attn_gain,
    mlp_gain,
    query_gain,
    key_gain,
    query_weight,
    key_matrix,
    value_matrix,
    output_weight,
    gate_weight,
    up_weight,
    down_weight,
    cotangent,
):
    seq_count, local_rows, width = tokens.shape
    seq_length = segments.shape[1]
    shard_rows = attn_gain.shape[0]
    head_rows = query_gain.shape[0]
    query_width = query_weight.shape[1]
    key_width = key_matrix.shape[1]
    hidden_units = gate_weight.shape[1]
    qkv_width = query_width + 2 * key_width
    me = lax.axis_index("tensor")
    swap = [(0, 1), (1, 0)]

    def rows_all(member):
        if n_tensor == 2:
            other = lax.ppermute(member, "tensor", swap)
            return jnp.concatenate(
                [jnp.where(me == 0, member, other), jnp.where(me == 0, other, member)], axis=1
            )
        return lax.all_gather(member, "tensor", axis=1, tiled=True)

    def rows_sum(member):
        member = member.reshape(seq_count, seq_length, width)
        if n_tensor == 2:
            lower, upper = member[:, :local_rows], member[:, local_rows:]
            sent = jnp.where(me == 0, upper, lower).astype(BF)
            kept = jnp.where(me == 0, lower, upper)
            return kept + lax.ppermute(sent, "tensor", swap).astype(F32)
        return lax.psum_scatter(member, "tensor", scatter_dimension=1, tiled=True)

    def flat(member):
        return member.reshape(seq_count * seq_length, -1)

    def column(vector):
        return jnp.pad(vector[:, None], ((0, shard_rows - vector.shape[0]), (0, 0)))

    gain_columns = jnp.concatenate(
        [column(member) for member in (attn_gain, mlp_gain, query_gain, key_gain)], axis=1
    )
    gain_columns = jnp.pad(gain_columns, ((0, 0), (0, LANES - 4)))
    first_shard = jnp.concatenate(
        [query_weight, key_matrix, value_matrix, output_weight.T, gain_columns], axis=1
    )
    second_shard = jnp.concatenate([gate_weight, up_weight, down_weight.T], axis=1)
    first_all = lax.all_gather(first_shard, "fsdp", axis=0, tiled=True)
    second_all = lax.all_gather(second_shard, "fsdp", axis=0, tiled=True)
    weight_qkv = first_all[:, :qkv_width]
    weight_out = first_all[:, qkv_width : qkv_width + query_width]
    gains = first_all[:, qkv_width + query_width :].astype(F32)
    gain_attn, gain_mlp = gains[:, 0], gains[:, 1]
    split_gains = gains.reshape(-1, shard_rows, LANES)[:, :head_rows]
    gain_query = split_gains[:, :, 2].reshape(1, -1)
    gain_key = split_gains[:, :, 3].reshape(1, -1)
    weight_gate = second_all[:, :hidden_units]
    weight_up = second_all[:, hidden_units : 2 * hidden_units]
    weight_down = second_all[:, 2 * hidden_units :]
    head_dim = gain_query.shape[1]

    tokens_all = rows_all(tokens)
    cotangent_all = flat(rows_all(cotangent))
    starts = starts_of(segments)
    positions = jnp.arange(seq_length, dtype=jnp.int32) - starts
    cosine_table, sine_table = rope_tables(positions, head_dim)
    tables = (
        flat(cosine_table),
        flat(sine_table),
        starts.reshape(seq_count, 1, seq_length),
        gain_query,
        gain_key,
    )

    source = tokens.astype(F32)
    inverse_one = scale_of(source)
    normed_one = source * inverse_one
    source_all = flat(tokens_all.astype(F32))
    normed_all = source_all * scale_of(source_all)
    first_hidden = (normed_all * gain_attn).astype(BF)
    qkv = nn(first_hidden, weight_qkv)
    attended = attend_forward(qkv, tables, seq_count, query_width, key_width)
    middle = source + rows_sum(nt(attended, weight_out))
    inverse_two = scale_of(middle)
    normed_two = middle * inverse_two
    second_hidden = flat(rows_all((normed_two * gain_mlp).astype(BF)))

    gate_value = nn(second_hidden, weight_gate)
    up_projected = nn(second_hidden, weight_up)
    sigmoid_gate = jax.nn.sigmoid(gate_value)
    silu_gate = gate_value * sigmoid_gate
    active = (silu_gate * up_projected).astype(BF)
    active_gradient = nn(cotangent_all, weight_down)
    gate_rows = (
        active_gradient * up_projected * (sigmoid_gate * (1.0 + gate_value * (1.0 - sigmoid_gate)))
    ).astype(BF)
    up_rows = (active_gradient * silu_gate).astype(BF)
    hidden_two_part = nt(gate_rows, weight_gate) + nt(up_rows, weight_up)
    dsecond = rows_sum(hidden_two_part)
    layer_out = (middle + rows_sum(nt(active, weight_down))).astype(BF)

    mlp_gain_part = jnp.sum(dsecond * normed_two, axis=(0, 1))
    shaped = dsecond * gain_mlp
    back_two = inverse_two * (
        shaped - normed_two * jnp.mean(shaped * normed_two, axis=-1, keepdims=True)
    )
    grad_middle = cotangent.astype(F32) + back_two

    mlp_grads = jnp.concatenate(
        [
            tn(second_hidden, gate_rows).astype(BF),
            tn(second_hidden, up_rows).astype(BF),
            tn(cotangent_all, active).astype(BF),
        ],
        axis=1,
    )
    mlp_sums = lax.psum_scatter(mlp_grads, "fsdp", scatter_dimension=0, tiled=True)

    attention_gradient = flat(rows_all(grad_middle.astype(BF)))
    grad_mixed = nn(attention_gradient, weight_out).astype(BF)
    query_back, key_back, value_back, head_gains = attend_backward(
        qkv, grad_mixed, tables, seq_count, query_width, key_width
    )
    qkv_back = jnp.concatenate([query_back, key_back, value_back], axis=1)
    hidden_one_part = nt(qkv_back, weight_qkv)
    attn_gain_part = jnp.sum(hidden_one_part * normed_all, axis=0)
    head_gains = jnp.sum(head_gains, axis=(0, 1))

    def spread(vector):
        split = vector.reshape(-1, head_rows)
        return jnp.pad(split, ((0, 0), (0, shard_rows - head_rows))).reshape(-1)

    gain_parts = jnp.stack(
        [attn_gain_part, mlp_gain_part, spread(head_gains[0]), spread(head_gains[1])], axis=1
    )
    attention_grads = jnp.concatenate(
        [
            tn(first_hidden, qkv_back).astype(BF),
            tn(attention_gradient, attended).astype(BF),
            jnp.pad(gain_parts, ((0, 0), (0, LANES - 4))).astype(BF),
        ],
        axis=1,
    )
    attention_sums = lax.psum_scatter(
        attention_grads, "fsdp", scatter_dimension=0, tiled=True
    ).astype(F32)
    gain_sums = lax.psum(attention_sums[:, qkv_width + query_width :], "tensor") if (
        n_tensor != 2
    ) else attention_sums[:, qkv_width + query_width :] + lax.ppermute(
        attention_sums[:, qkv_width + query_width :], "tensor", swap
    )

    dhidden = rows_sum(hidden_one_part)
    shaped = dhidden * gain_attn
    back_one = inverse_one * (
        shaped - normed_one * jnp.mean(shaped * normed_one, axis=-1, keepdims=True)
    )
    grad_tokens = grad_middle + back_one
    mlp_sums = mlp_sums.astype(F32)
    return (
        layer_out,
        grad_tokens,
        gain_sums[:, 0],
        gain_sums[:, 1],
        gain_sums[:head_rows, 2],
        gain_sums[:head_rows, 3],
        attention_sums[:, :query_width],
        attention_sums[:, query_width : query_width + key_width],
        attention_sums[:, query_width + key_width : qkv_width],
        attention_sums[:, qkv_width : qkv_width + query_width].T,
        mlp_sums[:, :hidden_units],
        mlp_sums[:, hidden_units : 2 * hidden_units],
        mlp_sums[:, 2 * hidden_units :].T,
    )


def solution(mesh):
    split = P("fsdp", "tensor")
    turned = P("tensor", "fsdp")
    rows = P("fsdp", "tensor", None)
    vector = P("fsdp")
    in_specs = (rows, P("fsdp", None), vector, vector, vector, vector)
    in_specs = in_specs + (split, split, split, turned, split, split, turned, rows)
    out_specs = (rows, rows, vector, vector, vector, vector)
    out_specs = out_specs + (split, split, split, turned, split, split, turned)
    return jax.shard_map(
        functools.partial(local, mesh.shape["tensor"]),
        mesh=mesh,
        in_specs=in_specs,
        out_specs=out_specs,
        check_vma=False,
    )
```

time: 1410 us -> 589 us (0.42)
  waiting for transfers between devices: 986 us -> 321 us
  matrix products: 215 us -> 88.7 us
  Pallas kernels: 0 us -> 84.9 us
  blocking collectives: 75.3 us -> 0 us
  other arithmetic: 87.6 us -> 34.9 us
    reduce_scatter x11 -> x2, waiting for transfers between devices: 662 us -> 121 us  [the longest x1 106 us: local(): lax.psum_scatter(mlp_grads, 'fsdp', scatter_dimension=0, tiled=True)]
    all_gather x11 -> x2, waiting for transfers between devices: 319 us -> 34.8 us  [the longest x1 34.8 us: local(): first_all = lax.all_gather(first_shard, 'fsdp', axis=0, tiled=True)]
    ppermute x0 -> x9, waiting for transfers between devices: none -> 165 us  [the longest x4 83.3 us: rows_sum(): return kept + lax.ppermute(sent, 'tensor', swap).astype(F32)]
    dot_general x27 -> x15, matrix products: 215 us -> 88.7 us  [the longest x5 38.1 us: nn(): return jnp.dot(left, right, preferred_element_type=F32)]
    pallas_call x0 -> x2, Pallas kernels: none -> 84.9 us  [the longest x1 62.3 us: attend_backward(): pl.pallas_call(functools.partial(backward_kernel, group, block), grid=(se...]
    unnamed x2 -> x0, blocking collectives: 69.9 us -> none
    convert_element_type x13 -> x10, other arithmetic: 45 us -> 7.26 us  [the longest x4 3.19 us: rows_sum(): sent = jnp.where(me == 0, upper, lower).astype(BF)]
    reduce_sum x5 -> x3, other arithmetic: 22.8 us -> 1.55 us  [the longest x1 0.85 us: local(): mlp_gain_part = jnp.sum(dsecond * normed_two, axis=(0, 1))]
  transfers between devices with their start and end apart: 22 -> 13, of which waited for: 19 -> 11; matrix products, arithmetic and copies ran while one was open for 11% -> 11% of each run, Pallas kernels for 0% -> 4%
where the time goes in v1:
time: 589 us; the launch traced here: 580 us
  waiting for transfers between devices  321 us (54%)
  matrix products  88.7 us (15%)
  Pallas kernels  84.9 us (14%)
  other arithmetic  34.9 us (6%)
  local copies, waits for them, and re-layouts  22 us (4%)
  between operations  14.7 us (2%)
  starting transfers between devices  14 us (2%)
    reduce_scatter x1, waiting for transfers between devices, local(): lax.psum_scatter(mlp_grads, 'fsdp', scatter_dimension=0, tiled=True)  106 us
    ppermute x4, waiting for transfers between devices, rows_sum(): return kept + lax.ppermute(sent, 'tensor', swap).astype(F32)  83.3 us
    ppermute x4, waiting for transfers between devices, rows_all(): other = lax.ppermute(member, 'tensor', swap)  81.7 us
    pallas_call x1, Pallas kernels, attend_backward(): pl.pallas_call(functools.partial(backward_kernel, group, block), grid=(se...  62.3 us
    dot_general x5, matrix products, nn(): return jnp.dot(left, right, preferred_element_type=F32)  38.1 us
    all_gather x1, waiting for transfers between devices, local(): first_all = lax.all_gather(first_shard, 'fsdp', axis=0, tiled=True)  34.8 us
    dot_general x5, matrix products, tn(): lax.dot_general(left, right, (((0,), (0,)), ((), ())), preferred_element_...  25.8 us
    dot_general x5, matrix products, nt(): lax.dot_general(left, right, (((1,), (1,)), ((), ())), preferred_element_...  24.8 us
  transfers between devices with their start and end apart: 13, of which 11 were waited for; matrix products, arithmetic and copies ran while one was open for 11% of the time, Pallas kernels for 4%

profile of v1, /device:TPU:0, one launch (start us, length us, event | category | flops | bytes accessed | tf_op | source)
XLA Modules:
  0.0 580.3 jit_solution(5752588673680304389)
XLA Ops:
  14.5 3.0 collective-permute-start
  21.5 19.4 %collective-permute-done = bf16[1,512,1024]{2,1,0:T(8,128)(2,1)} collective-permute-done((bf16[1,512,1024]{2,1,0:T(8,128)(2,1)}, bf16[1,512,1024]{2,1,0:T(8,128)(2,1)}, u32[]{:S(2)}, u32[]{:S(2)}) %collective-permute-start) | collective-permute-done | bytes 1048608 | tf_op jit(solution)/shard_map/ppermute | solution.py:279
  43.8 34.8 %all-gather.3.cloned.1.call-done = bf16[1024,3200]{1,0:T(8,128)(2,1)} async-done(((bf16[64,3200]{1,0:T(8,128)(2,1)}), bf16[1024,3200]{1,0:T(8,128)(2,1)}) %all-gather.3.cloned.1.call-update) | async-done | bytes 6553616 | tf_op jit(solution)/shard_map/all_gather | solution.py:308
  80.5 6.7 %fusion.10.q_ref.k_ref.v_ref = f32[1024,2048]{1,0:T(8,128)S(1)} fusion(bf16[1024,3200]{1,0:T(8,128)(2,1)} %all-gather.3.cloned.1.call-done, f32[1024]{0:T(1024)S(1)} %get-tuple-element.24, f32[1024]{0:T(1024)S(1)} %add_rsqrt_fusion, bf16[512,1024]{1,0:T(8,128)(2,1)} %copy-done.15, bf16[512,1024]{1,0:T(8,128)(2,1)S(1)} %get-tuple-element.47), kind=kOutput, calls=%fused_computation.23 | convolution fusion | flops 4302307328 | bytes 14688256 | tf_op jit(solution)/shard_map/dot_general | solution.py:51
  87.2 22.6 %shard_map.237 = bf16[1024,1024]{1,0:T(8,128)(2,1)S(1)} custom-call(f32[1024,2048]{1,0:T(8,128)S(1)} %fusion.10.q_ref.k_ref.v_ref, f32[1024,2048]{1,0:T(8,128)S(1)} %fusion.10.q_ref.k_ref.v_ref, f32[1024,2048]{1,0:T(8,128)S(1)} %fusion.10.q_ref.k_ref.v_ref, f32[1024,128]{1,0:T(8,128)S(1)} %get-tuple-element.59.cos_ref, ...), custom_call_target="tpu_custom_call" | custom-call | flops 3221225472 | bytes 10485760 | tf_op jit(solution)/shard_map/pallas_call | solution.py:198
  109.8 4.0 convolution_bitcast_fusion
  116.5 23.6 %collective-permute-done.1 = bf16[1,512,1024]{2,1,0:T(8,128)(2,1)S(1)} collective-permute-done((bf16[1,512,1024]{2,1,0:T(8,128)(2,1)S(1)}, bf16[1,512,1024]{2,1,0:T(8,128)(2,1)S(1)}, u32[]{:S(2)}, u32[]{:S(2)}) %collective-permute-start.1) | collective-permute-done | bytes 1048608 | tf_op jit(solution)/shard_map/ppermute | solution.py:291
  142.6 20.0 %collective-permute-done.4 = bf16[1,512,1024]{2,1,0:T(8,128)(2,1)S(1)} collective-permute-done((bf16[1,512,1024]{2,1,0:T(8,128)(2,1)S(1)}, bf16[1,512,1024]{2,1,0:T(8,128)(2,1)S(1)}, u32[]{:S(2)}, u32[]{:S(2)}) %collective-permute-start.4) | collective-permute-done | bytes 1048608 | tf_op jit(solution)/shard_map/ppermute | solution.py:279
  164.0 20.3 %collective-permute-done.2 = bf16[1,512,1024]{2,1,0:T(8,128)(2,1)S(1)} collective-permute-done((bf16[1,512,1024]{2,1,0:T(8,128)(2,1)S(1)}, bf16[1,512,1024]{2,1,0:T(8,128)(2,1)S(1)}, u32[]{:S(2)}, u32[]{:S(2)}) %collective-permute-start.2) | collective-permute-done | bytes 1048608 | tf_op jit(solution)/shard_map/ppermute | solution.py:279
  186.1 8.8 %fusion.12 = f32[1024,1536]{1,0:T(8,128)} fusion(bf16[1024,4608]{1,0:T(8,128)(2,1)} %all-gather.5.cloned.1.call-done, bf16[1,512,1024]{2,1,0:T(8,128)(2,1)} %get-tuple-element.44, bf16[1,512,1024]{2,1,0:T(8,128)(2,1)} %get-tuple-element.43), kind=kOutput, calls=%fused_computation.28 | convolution fusion | flops 3225419776 | bytes 11534336 | tf_op jit(solution)/shard_map/dot_general | solution.py:51
  195.0 5.4 fusion.18
  200.3 11.9 %multiply_convert_fusion.1 = (bf16[1024,1536]{1,0:T(8,128)(2,1)}, bf16[1024,1536]{1,0:T(8,128)(2,1)}, bf16[1024,1536]{1,0:T(8,128)(2,1)}) fusion(f32[1024,1536]{1,0:T(8,128)} %fusion.12, f32[1024,1536]{1,0:T(8,128)} %fusion.18, bf16[1024,4608]{1,0:T(8,128)(2,1)S(1)} %copy-done.26, bf16[1,512,1024]{2,1,0:T(8,128)(2,1)S(1)} %copy-done.23, ...), kind=kOutput, calls=%fused_computation.5 | convolution fusion | flops 3249012736 | bytes 27262976 | tf_op jit(solution)/shard_map/dot_general | solution.py:51
  212.3 5.5 fusion.16
  217.8 3.5 add_bitcast_fusion
  223.1 23.0 %collective-permute-done.5 = bf16[1,512,1024]{2,1,0:T(8,128)(2,1)S(1)} collective-permute-done((bf16[1,512,1024]{2,1,0:T(8,128)(2,1)S(1)}, bf16[1,512,1024]{2,1,0:T(8,128)(2,1)S(1)}, u32[]{:S(2)}, u32[]{:S(2)}) %collective-permute-start.5) | collective-permute-done | bytes 1048608 | tf_op jit(solution)/shard_map/ppermute | solution.py:291
  249.8 22.0 %collective-permute-done.6 = bf16[1,512,1024]{2,1,0:T(8,128)(2,1)S(1)} collective-permute-done((bf16[1,512,1024]{2,1,0:T(8,128)(2,1)S(1)}, bf16[1,512,1024]{2,1,0:T(8,128)(2,1)S(1)}, u32[]{:S(2)}, u32[]{:S(2)}) %collective-permute-start.6) | collective-permute-done | bytes 1048608 | tf_op jit(solution)/shard_map/ppermute | solution.py:279
  272.1 3.8 convolution_convert_fusion.4
  275.9 5.3 convolution_convert_fusion.5.grad_ref
  281.1 62.3 %shard_map.238 = (bf16[1024,1024]{1,0:T(8,128)(2,1)S(1)}, bf16[1024,512]{1,0:T(8,128)(2,1)S(1)}, bf16[1024,512]{1,0:T(8,128)(2,1)S(1)}, f32[1,4,2,128]{3,2,1,0:T(2,128)S(1)}) custom-call(f32[1024,2048]{1,0:T(8,128)} %copy-done, f32[1024,2048]{1,0:T(8,128)} %copy-done, f32[1024,2048]{1,0:T(8,128)} %copy-done, ...), custom_call_target="tpu_custom_call" | custom-call | flops 7516192768 | bytes 14680064 | tf_op jit(solution)/shard_map/pallas_call | solution.py:223
  347.6 8.9 %convolution_convert_fusion.3 = bf16[1024,2048]{1,0:T(8,128)(2,1)} fusion(bf16[1024,2048]{1,0:T(8,128)(2,1)} %constant_dynamic-update-slice_fusion.4, f32[1024]{0:T(1024)S(1)} %get-tuple-element.24, f32[1024]{0:T(1024)S(1)} %add_rsqrt_fusion, bf16[512,1024]{1,0:T(8,128)(2,1)S(1)} %copy-done.16, bf16[512,1024]{1,0:T(8,128)(2,1)S(1)} %copy-done.14), kind=kOutput, calls=%fused_computation.20 | convolution fusion | flops 4304404480 | bytes 10493952 | tf_op jit(solution)/shard_map/dot_general | solution.py:55
  356.6 6.4 %fusion.6 = (bf16[1024]{0:T(1024)(128)(2,1)S(1)}, f32[1024,1024]{1,0:T(8,128)}) fusion(f32[1024]{0:T(1024)S(1)} %add_rsqrt_fusion, bf16[512,1024]{1,0:T(8,128)(2,1)S(1)} %copy-done.16, bf16[512,1024]{1,0:T(8,128)(2,1)S(1)} %copy-done.14, bf16[1024,2048]{1,0:T(8,128)(2,1)S(1)} %copy-done.20, bf16[1024,3200]{1,0:T(8,128)(2,1)S(1)} %bitcast.76), kind=kOutput, calls=%fused_computation.14 | convolution fusion | flops 4302306304 | bytes 14686208 | tf_op jit(solution)/shard_map/dot_general | solution.py:47
  363.2 5.5 fusion.1
  370.3 5.7 convolution_convert_fusion.1
  376.1 3.7 convolution_convert_fusion.2
  379.8 3.7 convolution_convert_fusion
  383.5 5.0 pad_maximum_fusion
  392.9 5.5 fusion.26
  399.2 18.2 %collective-permute-done.7 = bf16[1,512,1024]{2,1,0:T(8,128)(2,1)S(1)} collective-permute-done((bf16[1,512,1024]{2,1,0:T(8,128)(2,1)S(1)}, bf16[1,512,1024]{2,1,0:T(8,128)(2,1)S(1)}, u32[]{:S(2)}, u32[]{:S(2)}) %collective-permute-start.7) | collective-permute-done | bytes 1048608 | tf_op jit(solution)/shard_map/ppermute | solution.py:291
  418.1 18.6 %collective-permute-done.3 = bf16[1,512,1024]{2,1,0:T(8,128)(2,1)S(1)} collective-permute-done((bf16[1,512,1024]{2,1,0:T(8,128)(2,1)S(1)}, bf16[1,512,1024]{2,1,0:T(8,128)(2,1)S(1)}, u32[]{:S(2)}, u32[]{:S(2)}) %collective-permute-start.3) | collective-permute-done | bytes 1048608 | tf_op jit(solution)/shard_map/ppermute | solution.py:291
  436.7 3.0 fusion.32
  439.7 14.9 %reduce-scatter.3.cloned.1.call-done = bf16[64,3200]{1,0:T(8,128)(2,1)} async-done(((bf16[1024,3200]{1,0:T(8,128)(2,1)}), bf16[64,3200]{1,0:T(8,128)(2,1)}) %reduce-scatter.3.cloned.1.call-update) | async-done | bytes 409616 | tf_op jit(solution)/shard_map/reduce_scatter | solution.py:404
  463.2 106.3 %reduce-scatter.5.cloned.1.call-done = bf16[64,4608]{1,0:T(8,128)(2,1)} async-done(((bf16[1024,4608]{1,0:T(8,128)(2,1)}), bf16[64,4608]{1,0:T(8,128)(2,1)}) %reduce-scatter.5.cloned.1.call-update) | async-done | bytes 589840 | tf_op jit(solution)/shard_map/reduce_scatter | solution.py:377
  (156 shorter events, 54.4 us)
Async XLA Ops:
  7.2 71.4 %all-gather.3.cloned.1.call-start = ((), (), s32[]{:S(2)}) async-start(), calls=%async_computation.2 | async-start | bytes 6963200 | tf_op jit(solution)/shard_map/all_gather | solution.py:308
  11.6 29.4 %copy-start.7 = (bf16[1,512,1024]{2,1,0:T(8,128)(2,1)S(1)}, bf16[1,512,1024]{2,1,0:T(8,128)(2,1)}, u32[]{:S(2)}) copy-start(bf16[1,512,1024]{2,1,0:T(8,128)(2,1)} %param.14) | copy-start | bytes 3145732
  12.4 173.8 %all-gather.5.cloned.1.call-start = ((), (), s32[]{:S(2)}) async-start(), calls=%async_computation.3 | async-start | bytes 10027008 | tf_op jit(solution)/shard_map/all_gather | solution.py:309
  14.4 440.1 %reduce-scatter.3.cloned.1.call-start = ((), (), s32[]{:S(2)}) async-start(), calls=%async_computation.4 | async-start | bytes 6963200 | tf_op jit(solution)/shard_map/reduce_scatter | solution.py:404
  14.5 26.5 %collective-permute-start = (bf16[1,512,1024]{2,1,0:T(8,128)(2,1)}, bf16[1,512,1024]{2,1,0:T(8,128)(2,1)}, u32[]{:S(2)}, u32[]{:S(2)}) collective-permute-start(bf16[1,512,1024]{2,1,0:T(8,128)(2,1)} %param.14), channel_id=1, source_target_pairs={{0,1},{1,0},{2,3},{3,2},{4,5},{5,4},{6,7},{7,6},{8,9},{9,8},{10,11... | collective-permute-start | bytes 3145736 | tf_op jit(solution)/shard_map/ppermute | solution.py:279
  42.4 44.8 %copy-start.13 = (bf16[512,1024]{1,0:T(8,128)(2,1)}, bf16[512,1024]{1,0:T(8,128)(2,1)S(1)}, u32[]{:S(2)}) copy-start(bf16[512,1024]{1,0:T(8,128)(2,1)S(1)} %get-tuple-element.47) | copy-start | bytes 3145732
  87.2 22.6 %copy-start = (f32[1024,2048]{1,0:T(8,128)}, f32[1024,2048]{1,0:T(8,128)S(1)}, u32[]{:S(2)}) copy-start(f32[1024,2048]{1,0:T(8,128)S(1)} %fusion.10.q_ref.k_ref.v_ref) | copy-start | bytes 25165828
  113.8 26.3 %copy-start.8 = (bf16[1,512,1024]{2,1,0:T(8,128)(2,1)S(1)}, bf16[1,512,1024]{2,1,0:T(8,128)(2,1)}, u32[]{:S(2)}) copy-start(bf16[1,512,1024]{2,1,0:T(8,128)(2,1)} %param.14) | copy-start | bytes 3145732
  114.0 26.1 %collective-permute-start.1 = (bf16[1,512,1024]{2,1,0:T(8,128)(2,1)S(1)}, bf16[1,512,1024]{2,1,0:T(8,128)(2,1)S(1)}, u32[]{:S(2)}, u32[]{:S(2)}) collective-permute-start(bf16[1,512,1024]{2,1,0:T(8,128)(2,1)S(1)} %select_convert_fusion.3), channel_id=1, source_target_pairs={{0,1},{1,0},{2,3},{3,2},{4,5},{5,4},{6,7},{7,6},{8,9},{9,8},{10,11... | collective-permute-start | bytes 3145736 | tf_op jit(solution)/shard_map/ppermute | solution.py:291
  115.5 47.0 %collective-permute-start.4 = (bf16[1,512,1024]{2,1,0:T(8,128)(2,1)S(1)}, bf16[1,512,1024]{2,1,0:T(8,128)(2,1)S(1)}, u32[]{:S(2)}, u32[]{:S(2)}) collective-permute-start(bf16[1,512,1024]{2,1,0:T(8,128)(2,1)S(1)} %copy-done.10), channel_id=1, source_target_pairs={{0,1},{1,0},{2,3},{3,2},{4,5},{5,4},{6,7},{7,6},{8,9},{9,8},{10,11... | collective-permute-start | bytes 3145736 | tf_op jit(solution)/shard_map/ppermute | solution.py:279
  140.8 43.6 %copy-start.1 = (f32[1,512,1024]{2,1,0:T(8,128)}, f32[1,512,1024]{2,1,0:T(8,128)S(1)}, u32[]{:S(2)}) copy-start(f32[1,512,1024]{2,1,0:T(8,128)S(1)} %get-tuple-element.35) | copy-start | bytes 6291460
  141.0 43.3 %collective-permute-start.2 = (bf16[1,512,1024]{2,1,0:T(8,128)(2,1)S(1)}, bf16[1,512,1024]{2,1,0:T(8,128)(2,1)S(1)}, u32[]{:S(2)}, u32[]{:S(2)}) collective-permute-start(bf16[1,512,1024]{2,1,0:T(8,128)(2,1)S(1)} %multiply_convert_fusion.3), channel_id=1, source_target_pairs={{0,1},{1,0},{2,3},{3,2},{4,5},{5,4},{6,7},{7,6},{8,9},{9,8},{10,11... | collective-permute-start | bytes 3145736 | tf_op jit(solution)/shard_map/ppermute | solution.py:279
  186.1 8.8 %copy-start.21 = (bf16[1,512,1024]{2,1,0:T(8,128)(2,1)S(1)}, bf16[1,512,1024]{2,1,0:T(8,128)(2,1)}, u32[]{:S(2)}) copy-start(bf16[1,512,1024]{2,1,0:T(8,128)(2,1)} %get-tuple-element.45) | copy-start | bytes 3145732
  186.1 8.8 %copy-start.23 = (bf16[1,512,1024]{2,1,0:T(8,128)(2,1)S(1)}, bf16[1,512,1024]{2,1,0:T(8,128)(2,1)}, u32[]{:S(2)}) copy-start(bf16[1,512,1024]{2,1,0:T(8,128)(2,1)} %get-tuple-element.46) | copy-start | bytes 3145732
  186.1 8.8 %copy-start.26 = (bf16[1024,4608]{1,0:T(8,128)(2,1)S(1)}, bf16[1024,4608]{1,0:T(8,128)(2,1)}, u32[]{:S(2)}) copy-start(bf16[1024,4608]{1,0:T(8,128)(2,1)} %all-gather.5.cloned.1.call-done) | copy-start | bytes 28311556
  221.3 24.8 %copy-start.2 = (f32[1,512,1024]{2,1,0:T(8,128)S(1)}, f32[1,512,1024]{2,1,0:T(8,128)}, u32[]{:S(2)}) copy-start(f32[1,512,1024]{2,1,0:T(8,128)} %copy-done.1) | copy-start | bytes 6291460
  221.5 25.4 %copy-start.11 = (bf16[1,512,1024]{2,1,0:T(8,128)(2,1)S(1)}, bf16[1,512,1024]{2,1,0:T(8,128)(2,1)}, u32[]{:S(2)}) copy-start(bf16[1,512,1024]{2,1,0:T(8,128)(2,1)} %param.27) | copy-start | bytes 3145732
  221.5 24.5 %collective-permute-start.5 = (bf16[1,512,1024]{2,1,0:T(8,128)(2,1)S(1)}, bf16[1,512,1024]{2,1,0:T(8,128)(2,1)S(1)}, u32[]{:S(2)}, u32[]{:S(2)}) collective-permute-start(bf16[1,512,1024]{2,1,0:T(8,128)(2,1)S(1)} %select_convert_fusion.1), channel_id=1, source_target_pairs={{0,1},{1,0},{2,3},{3,2},{4,5},{5,4},{6,7},{7,6},{8,9},{9,8},{10,11... | collective-permute-start | bytes 3145736 | tf_op jit(solution)/shard_map/ppermute | solution.py:291
  248.3 23.6 %collective-permute-start.6 = (bf16[1,512,1024]{2,1,0:T(8,128)(2,1)S(1)}, bf16[1,512,1024]{2,1,0:T(8,128)(2,1)S(1)}, u32[]{:S(2)}, u32[]{:S(2)}) collective-permute-start(bf16[1,512,1024]{2,1,0:T(8,128)(2,1)S(1)} %fusion.52), channel_id=1, source_target_pairs={{0,1},{1,0},{2,3},{3,2},{4,5},{5,4},{6,7},{7,6},{8,9},{9,8},{10,11... | collective-permute-start | bytes 3145736 | tf_op jit(solution)/shard_map/ppermute | solution.py:279
  345.4 11.1 %slice-start = ((s8[6553600]{0:T(1024)(128)(4,1)}), s8[4194304]{0:T(1024)(128)(4,1)S(1)}, s32[]{:S(2)}) async-start(s8[6553600]{0:T(1024)(128)(4,1)} %bitcast.75), calls=%async_computation.6 | async-start | bytes 8388608
  347.6 8.9 %copy-start.20 = (bf16[1024,2048]{1,0:T(8,128)(2,1)S(1)}, bf16[1024,2048]{1,0:T(8,128)(2,1)}, u32[]{:S(2)}) copy-start(bf16[1024,2048]{1,0:T(8,128)(2,1)} %constant_dynamic-update-slice_fusion.4) | copy-start | bytes 12582916
  347.6 8.9 %slice-start.1 = ((s8[6553600]{0:T(1024)(128)(4,1)}), s8[2359296]{0:T(1024)(128)(4,1)S(1)}, s32[]{:S(2)}) async-start(s8[6553600]{0:T(1024)(128)(4,1)} %bitcast.75), calls=%async_computation.7 | async-start | bytes 4718592
  356.6 6.7 %copy-start.17 = (bf16[1024,1024]{1,0:T(8,128)(2,1)S(1)}, bf16[1024,1024]{1,0:T(8,128)(2,1)}, u32[]{:S(2)}) copy-start(bf16[1024,1024]{1,0:T(8,128)(2,1)} %convolution_convert_fusion.4) | copy-start | bytes 6291460
  368.8 200.7 %reduce-scatter.5.cloned.1.call-start = ((), (), s32[]{:S(2)}) async-start(), calls=%async_computation.5 | async-start | bytes 10027008 | tf_op jit(solution)/shard_map/reduce_scatter | solution.py:377
  391.2 26.2 %collective-permute-start.7 = (bf16[1,512,1024]{2,1,0:T(8,128)(2,1)S(1)}, bf16[1,512,1024]{2,1,0:T(8,128)(2,1)S(1)}, u32[]{:S(2)}, u32[]{:S(2)}) collective-permute-start(bf16[1,512,1024]{2,1,0:T(8,128)(2,1)S(1)} %select_convert_fusion), channel_id=1, source_target_pairs={{0,1},{1,0},{2,3},{3,2},{4,5},{5,4},{6,7},{7,6},{8,9},{9,8},{10,11... | collective-permute-start | bytes 3145736 | tf_op jit(solution)/shard_map/ppermute | solution.py:291
  392.9 24.5 %copy-start.4 = (f32[1024,1024]{1,0:T(8,128)S(1)}, f32[1024,1024]{1,0:T(8,128)}, u32[]{:S(2)}) copy-start(f32[1024,1024]{1,0:T(8,128)} %get-tuple-element.58) | copy-start | bytes 12582916
  398.4 19.0 %copy-start.9 = (bf16[1,512,1024]{2,1,0:T(8,128)(2,1)S(1)}, bf16[1,512,1024]{2,1,0:T(8,128)(2,1)}, u32[]{:S(2)}) copy-start(bf16[1,512,1024]{2,1,0:T(8,128)(2,1)} %param.14) | copy-start | bytes 3145732
  398.6 38.1 %collective-permute-start.3 = (bf16[1,512,1024]{2,1,0:T(8,128)(2,1)S(1)}, bf16[1,512,1024]{2,1,0:T(8,128)(2,1)S(1)}, u32[]{:S(2)}, u32[]{:S(2)}) collective-permute-start(bf16[1,512,1024]{2,1,0:T(8,128)(2,1)S(1)} %select_convert_fusion.2), channel_id=1, source_target_pairs={{0,1},{1,0},{2,3},{3,2},{4,5},{5,4},{6,7},{7,6},{8,9},{9,8},{10,11... | collective-permute-start | bytes 3145736 | tf_op jit(solution)/shard_map/ppermute | solution.py:291
  399.2 37.5 %copy-start.3 = (f32[1,512,1024]{2,1,0:T(8,128)S(1)}, f32[1,512,1024]{2,1,0:T(8,128)}, u32[]{:S(2)}) copy-start(f32[1,512,1024]{2,1,0:T(8,128)} %copy-done.1) | copy-start | bytes 6291460
  399.2 37.5 %copy-start.6 = (f32[1,512,1024]{2,1,0:T(8,128)S(1)}, f32[1,512,1024]{2,1,0:T(8,128)}, u32[]{:S(2)}) copy-start(f32[1,512,1024]{2,1,0:T(8,128)} %copy-done.5) | copy-start | bytes 6291460
  399.2 37.5 %copy-start.12 = (bf16[1,512,1024]{2,1,0:T(8,128)(2,1)S(1)}, bf16[1,512,1024]{2,1,0:T(8,128)(2,1)}, u32[]{:S(2)}) copy-start(bf16[1,512,1024]{2,1,0:T(8,128)(2,1)} %param.27) | copy-start | bytes 3145732
  455.3 6.5 %collective-permute-start.8 = (f32[64,128]{1,0:T(8,128)S(1)}, f32[64,128]{1,0:T(8,128)S(1)}, u32[]{:S(2)}, u32[]{:S(2)}) collective-permute-start(f32[64,128]{1,0:T(8,128)S(1)} %slice.168), channel_id=1, source_target_pairs={{0,1},{1,0},{2,3},{3,2},{4,5},{5,4},{6,7},{7,6},{8,9},{9,8},{10,11... | collective-permute-start | bytes 98312 | tf_op jit(solution)/shard_map/ppermute | solution.py:409
  (14 other events, 39.2 us)
Sparse Core Ops, SparseCore 0:
  12.5 66.0 all-gather.2
  80.9 79.9 all-gather.4
  368.9 85.6 reduce-scatter.2
  459.1 110.3 reduce-scatter.4

commit v2 on v1

--- a/solution.py
+++ b/solution.py
@@ -66,10 +66,10 @@
     return (gained * cosine + turn(gained) * sine).astype(BF), normed, inverse
 
 
-def scores_block(key_part, query_part, starts, first_row, scale):
+def scores_block(key_part, query_part, starts, key_first, query_first, scale):
     scores = nt(key_part, query_part) * scale
-    key_index = lax.broadcasted_iota(jnp.int32, scores.shape, 0)
-    query_index = lax.broadcasted_iota(jnp.int32, scores.shape, 1) + first_row
+    key_index = lax.broadcasted_iota(jnp.int32, scores.shape, 0) + key_first
+    query_index = lax.broadcasted_iota(jnp.int32, scores.shape, 1) + query_first
     allowed = (key_index <= query_index) & (key_index >= starts)
     return jnp.where(allowed, scores, -1000000000.0)
 
@@ -79,29 +79,66 @@
     return exponent * (1.0 / jnp.sum(exponent, axis=0, keepdims=True))
 
 
+def for_windows(begins_ref, block, grain, seq_length, body):
+    sequence = pl.program_id(0)
+    for first in range(0, seq_length, block):
+        tile = begins_ref[sequence, first // block] // grain
+        for lower in range(0, first + 1, grain):
+
+            @pl.when(tile == lower // grain)
+            def _(lower=lower, first=first):
+                body(lower, first, first + block)
+
+
 def forward_kernel(
-    group, block, q_ref, k_ref, v_ref, cos_ref, sin_ref, starts_ref, qg_ref, kg_ref, out_ref
+    group,
+    block,
+    grain,
+    begins_ref,
+    q_ref,
+    k_ref,
+    v_ref,
+    cos_ref,
+    sin_ref,
+    starts_ref,
+    qg_ref,
+    kg_ref,
+    out_ref,
+    key_rot,
+    value_turned,
+    query_rot,
 ):
     seq_length, head_dim = k_ref.shape
     scale = head_dim**-0.5
     cosine, sine = cos_ref[...], sin_ref[...]
-    key_rot, _, _ = prepared(k_ref[...], kg_ref[...], cosine, sine)
-    value_turned = v_ref[...].T.astype(BF)
-    for head in range(group):
-        columns = slice(head * head_dim, (head + 1) * head_dim)
-        query_rot, _, _ = prepared(q_ref[:, columns], qg_ref[...], cosine, sine)
-        for first in range(0, seq_length, block):
-            last = first + block
-            scores = scores_block(
-                key_rot[:last], query_rot[first:last], starts_ref[:, first:last], first, scale
-            )
-            probs = soft_block(scores).astype(BF)
-            out_ref[first:last, columns] = nn(value_turned[:, :last], probs).T.astype(BF)
+
+    @pl.when(pl.program_id(2) == 0)
+    def _():
+        key_rot[...] = prepared(k_ref[...], kg_ref[...], cosine, sine)[0]
+        value_turned[...] = v_ref[...].T.astype(BF)
+
+    query_rot[...] = prepared(q_ref[...], qg_ref[...], cosine, sine)[0]
+
+    def body(lower, first, last):
+        scores = scores_block(
+            key_rot[lower:last, :],
+            query_rot[first:last, :],
+            starts_ref[:, first:last],
+            lower,
+            first,
+            scale,
+        )
+        probs = soft_block(scores).astype(BF)
+        out_ref[first:last, :] = nn(value_turned[:, lower:last], probs).T.astype(BF)
+
+    for_windows(begins_ref, block, grain, seq_length, body)
 
 
 def backward_kernel(
     group,
     block,
+    grain,
+    begins_ref,
     q_ref,
     k_ref,
     v_ref,
@@ -118,14 +155,27 @@
     key_total,
     value_total,
     query_total,
+    key_rot,
+    key_turned,
+    value,
+    query_rot,
 ):
     seq_length, head_dim = k_ref.shape
     scale = head_dim**-0.5
     cosine, sine = cos_ref[...], sin_ref[...]
     key_gain, query_gain = kg_ref[...], qg_ref[...]
-    key_rot, key_normed, key_inverse = prepared(k_ref[...], key_gain, cosine, sine)
-    key_turned = key_rot.astype(F32).T.astype(BF)
-    value = v_ref[...].astype(BF)
+
+    @pl.when(pl.program_id(2) == 0)
+    def _():
+        rotated = prepared(k_ref[...], key_gain, cosine, sine)[0]
+        key_rot[...] = rotated
+        key_turned[...] = rotated.astype(F32).T.astype(BF)
+        value[...] = v_ref[...].astype(BF)
+        key_total[...] = jnp.zeros_like(key_total)
+        value_total[...] = jnp.zeros_like(value_total)
+
+    query_rotated, query_normed, query_inverse = prepared(q_ref[...], query_gain, cosine, sine)
+    query_rot[...] = query_rotated
 
     def norm_back(rounded, normed, inverse, gain):
         gradient = rounded.astype(BF).astype(F32)
@@ -135,37 +185,44 @@
         inner = jnp.mean(shaped * normed, axis=-1, keepdims=True)
         return (inverse * (shaped - normed * inner)).astype(BF), gain_grad
 
-    key_total[...] = jnp.zeros_like(key_total)
-    value_total[...] = jnp.zeros_like(value_total)
-    gain_total = jnp.zeros((1, head_dim), F32)
-    for head in range(group):
-        columns = slice(head * head_dim, (head + 1) * head_dim)
-        query_rot, query_normed, query_inverse = prepared(
-            q_ref[:, columns], query_gain, cosine, sine
+    def body(lower, first, last):
+        query_part = query_rot[first:last, :]
+        grad_part = grad_ref[first:last, :]
+        probs = soft_block(
+            scores_block(
+                key_rot[lower:last, :],
+                query_part,
+                starts_ref[:, first:last],
+                lower,
+                first,
+                scale,
+            )
         )
-        for first in range(0, seq_length, block):
-            last = first + block
-            query_part = query_rot[first:last]
-            grad_part = grad_ref[first:last, columns]
-            probs = soft_block(
-                scores_block(key_rot[:last], query_part, starts_ref[:, first:last], first, scale)
-            )
-            grad_probs = nt(value[:last], grad_part)
-            delta = jnp.sum(grad_probs * probs, axis=0, keepdims=True)
-            score_grad = (probs * (grad_probs - delta)).astype(BF)
-            value_total[:last, :] += nn(probs.astype(BF), grad_part)
-            key_total[:last, :] += nn(score_grad, query_part)
-            query_total[first:last, :] = nn(key_turned[:, :last], score_grad).T
-        query_back, gain_part = norm_back(
-            query_total[...] * scale, query_normed, query_inverse, query_gain
+        grad_probs = nt(value[lower:last, :], grad_part)
+        delta = jnp.sum(grad_probs * probs, axis=0, keepdims=True)
+        score_grad = (probs * (grad_probs - delta)).astype(BF)
+        value_total[lower:last, :] += nn(probs.astype(BF), grad_part)
+        key_total[lower:last, :] += nn(score_grad, query_part)
+        query_total[first:last, :] = nn(key_turned[:, lower:last], score_grad).T
+
+    for_windows(begins_ref, block, grain, seq_length, body)
+
+    query_back, gain_part = norm_back(
+        query_total[...] * scale, query_normed, query_inverse, query_gain
+    )
+    dq_ref[...] = query_back
+    gains_ref[0:1, :] = gain_part
+    gains_ref[1:2, :] = jnp.zeros_like(gain_part)
+
+    @pl.when(pl.program_id(2) == group - 1)
+    def _():
+        _, key_normed, key_inverse = prepared(k_ref[...], key_gain, cosine, sine)
+        key_back, key_gain_part = norm_back(
+            key_total[...] * scale, key_normed, key_inverse, key_gain
         )
-        dq_ref[:, columns] = query_back
-        gain_total = gain_total + gain_part
-    key_back, key_gain_part = norm_back(key_total[...] * scale, key_normed, key_inverse, key_gain)
-    dk_ref[...] = key_back
-    dv_ref[...] = value_total[...].astype(BF)
-    gains_ref[0:1, :] = gain_total
-    gains_ref[1:2, :] = key_gain_part
+        dk_ref[...] = key_back
+        dv_ref[...] = value_total[...].astype(BF)
+        gains_ref[1:2, :] = key_gain_part
 
 
 def attention_specs(seq_length, query_width, key_width, head_dim):
@@ -173,77 +230,99 @@
     group = query_width // key_width
     key_base = query_width // head_dim
     value_base = key_base + key_heads
+    wide = pl.BlockSpec((seq_length, head_dim), lambda s, h, g, b: (s, h * group + g))
+    narrow = pl.BlockSpec((seq_length, head_dim), lambda s, h, g, b: (s, h))
     raw = [
-        pl.BlockSpec((seq_length, group * head_dim), lambda s, h: (s, h)),
-        pl.BlockSpec((seq_length, head_dim), lambda s, h: (s, key_base + h)),
-        pl.BlockSpec((seq_length, head_dim), lambda s, h: (s, value_base + h)),
+        wide,
+        pl.BlockSpec((seq_length, head_dim), lambda s, h, g, b: (s, key_base + h)),
+        pl.BlockSpec((seq_length, head_dim), lambda s, h, g, b: (s, value_base + h)),
     ]
     tables = [
-        pl.BlockSpec((seq_length, head_dim), lambda s, h: (s, 0)),
-        pl.BlockSpec((seq_length, head_dim), lambda s, h: (s, 0)),
-        pl.BlockSpec((None, 1, seq_length), lambda s, h: (s, 0, 0)),
-        pl.BlockSpec((1, head_dim), lambda s, h: (0, 0)),
-        pl.BlockSpec((1, head_dim), lambda s, h: (0, 0)),
+        pl.BlockSpec((seq_length, head_dim), lambda s, h, g, b: (s, 0)),
+        pl.BlockSpec((seq_length, head_dim), lambda s, h, g, b: (s, 0)),
+        pl.BlockSpec((None, 1, seq_length), lambda s, h, g, b: (s, 0, 0)),
+        pl.BlockSpec((1, head_dim), lambda s, h, g, b: (0, 0)),
+        pl.BlockSpec((1, head_dim), lambda s, h, g, b: (0, 0)),
     ]
-    return raw, tables, group, key_heads
+    return raw, tables, wide, narrow, group, key_heads
+
+
+def attention_tiles(seq_length):
+    return min(256, seq_length), min(128, seq_length)
 
 
 def attend_forward(qkv, tables, seq_count, query_width, key_width):
     seq_length = qkv.shape[0] // seq_count
     head_dim = tables[0].shape[-1]
-    raw_specs, table_specs, group, key_heads = attention_specs(
+    raw_specs, table_specs, wide, _, group, key_heads = attention_specs(
         seq_length, query_width, key_width, head_dim
     )
-    block = min(256, seq_length)
+    block, grain = attention_tiles(seq_length)
+    begins = tables[2][:, 0, ::block]
     return pl.pallas_call(
-        functools.partial(forward_kernel, group, block),
-        grid=(seq_count, key_heads),
-        in_specs=raw_specs + table_specs,
-        out_specs=pl.BlockSpec((seq_length, group * head_dim), lambda s, h: (s, h)),
+        functools.partial(forward_kernel, group, block, grain),
+        grid_spec=pltpu.PrefetchScalarGridSpec(
+            num_scalar_prefetch=1,
+            grid=(seq_count, key_heads, group),
+            in_specs=raw_specs + table_specs,
+            out_specs=wide,
+            scratch_shapes=[
+                pltpu.VMEM((seq_length, head_dim), BF),
+                pltpu.VMEM((head_dim, seq_length), BF),
+                pltpu.VMEM((seq_length, head_dim), BF),
+            ],
+        ),
         out_shape=jax.ShapeDtypeStruct((qkv.shape[0], query_width), BF),
-        compiler_params=pltpu.CompilerParams(vmem_limit_bytes=40 * 2**20),
+        compiler_params=pltpu.CompilerParams(vmem_limit_bytes=32 * 2**20),
         cost_estimate=pl.CostEstimate(
-            flops=3 * seq_count * seq_length * seq_length * query_width,
+            flops=2 * seq_count * seq_length * seq_length * query_width,
             bytes_accessed=qkv.size * 4 + qkv.shape[0] * query_width * 2,
             transcendentals=seq_count * seq_length * seq_length * query_width // head_dim,
         ),
-    )(qkv, qkv, qkv, *tables)
+    )(begins, qkv, qkv, qkv, *tables)
 
 
 def attend_backward(qkv, grad_mixed, tables, seq_count, query_width, key_width):
     seq_length = qkv.shape[0] // seq_count
     head_dim = tables[0].shape[-1]
-    raw_specs, table_specs, group, key_heads = attention_specs(
+    raw_specs, table_specs, wide, narrow, group, key_heads = attention_specs(
         seq_length, query_width, key_width, head_dim
     )
-    block = min(256, seq_length)
+    block, grain = attention_tiles(seq_length)
+    begins = tables[2][:, 0, ::block]
     rows = qkv.shape[0]
-    wide = pl.BlockSpec((seq_length, group * head_dim), lambda s, h: (s, h))
-    narrow = pl.BlockSpec((seq_length, head_dim), lambda s, h: (s, h))
+    total = pltpu.VMEM((seq_length, head_dim), F32)
+    part = pltpu.VMEM((seq_length, head_dim), BF)
     return pl.pallas_call(
-        functools.partial(backward_kernel, group, block),
-        grid=(seq_count, key_heads),
-        in_specs=raw_specs + [wide] + table_specs,
-        out_specs=[
-            wide,
-            narrow,
-            narrow,
-            pl.BlockSpec((None, None, 2, head_dim), lambda s, h: (s, h, 0, 0)),
-        ],
+        functools.partial(backward_kernel, group, block, grain),
+        grid_spec=pltpu.PrefetchScalarGridSpec(
+            num_scalar_prefetch=1,
+            grid=(seq_count, key_heads, group),
+            in_specs=raw_specs + [wide] + table_specs,
+            out_specs=[
+                wide,
+                narrow,
+                narrow,
+                pl.BlockSpec(
+                    (None, None, 2, head_dim), lambda s, h, g, b: (s, h * group + g, 0, 0)
+                ),
+            ],
+            scratch_shapes=[total, total, total, part]
+            + [pltpu.VMEM((head_dim, seq_length), BF), part, part],
+        ),
         out_shape=[
             jax.ShapeDtypeStruct((rows, query_width), BF),
             jax.ShapeDtypeStruct((rows, key_width), BF),
             jax.ShapeDtypeStruct((rows, key_width), BF),
-            jax.ShapeDtypeStruct((seq_count, key_heads, 2, head_dim), F32),
+            jax.ShapeDtypeStruct((seq_count, key_heads * group, 2, head_dim), F32),
         ],
-        scratch_shapes=[pltpu.VMEM((seq_length, head_dim), F32)] * 3,
-        compiler_params=pltpu.CompilerParams(vmem_limit_bytes=48 * 2**20),
+        compiler_params=pltpu.CompilerParams(vmem_limit_bytes=32 * 2**20),
         cost_estimate=pl.CostEstimate(
-            flops=7 * seq_count * seq_length * seq_length * query_width,
+            flops=5 * seq_count * seq_length * seq_length * query_width,
             bytes_accessed=qkv.size * 6 + rows * query_width * 2,
             transcendentals=seq_count * seq_length * seq_length * query_width // head_dim,
         ),
-    )(qkv, qkv, qkv, grad_mixed, *tables)
+    )(begins, qkv, qkv, qkv, grad_mixed, *tables)
 
 
 def local(
@@ -291,6 +370,9 @@
             return kept + lax.ppermute(sent, "tensor", swap).astype(F32)
         return lax.psum_scatter(member, "tensor", scatter_dimension=1, tiled=True)
 
+    def sum_shards(member):
+        return lax.psum_scatter(member, "fsdp", scatter_dimension=0, tiled=True)
+
     def flat(member):
         return member.reshape(seq_count * seq_length, -1)
 
@@ -319,8 +401,8 @@
     weight_down = second_all[:, 2 * hidden_units :]
     head_dim = gain_query.shape[1]
 
-    tokens_all = rows_all(tokens)
-    cotangent_all = flat(rows_all(cotangent))
+    tokens_all, cotangent_all = lax.optimization_barrier((rows_all(tokens), rows_all(cotangent)))
+    cotangent_all = flat(cotangent_all)
     starts = starts_of(segments)
     positions = jnp.arange(seq_length, dtype=jnp.int32) - starts
     cosine_table, sine_table = rope_tables(positions, head_dim)
@@ -356,16 +438,6 @@
     ).astype(BF)
     up_rows = (active_gradient * silu_gate).astype(BF)
     hidden_two_part = nt(gate_rows, weight_gate) + nt(up_rows, weight_up)
-    dsecond = rows_sum(hidden_two_part)
-    layer_out = (middle + rows_sum(nt(active, weight_down))).astype(BF)
-
-    mlp_gain_part = jnp.sum(dsecond * normed_two, axis=(0, 1))
-    shaped = dsecond * gain_mlp
-    back_two = inverse_two * (
-        shaped - normed_two * jnp.mean(shaped * normed_two, axis=-1, keepdims=True)
-    )
-    grad_middle = cotangent.astype(F32) + back_two
-
     mlp_grads = jnp.concatenate(
         [
             tn(second_hidden, gate_rows).astype(BF),
@@ -374,7 +446,16 @@
         ],
         axis=1,
     )
-    mlp_sums = lax.psum_scatter(mlp_grads, "fsdp", scatter_dimension=0, tiled=True)
+    dsecond, mlp_grads = lax.optimization_barrier((rows_sum(hidden_two_part), mlp_grads))
+    mlp_sums = sum_shards(mlp_grads)
+    layer_out = (middle + rows_sum(nt(active, weight_down))).astype(BF)
+
+    mlp_gain_part = jnp.sum(dsecond * normed_two, axis=(0, 1))
+    shaped = dsecond * gain_mlp
+    back_two = inverse_two * (
+        shaped - normed_two * jnp.mean(shaped * normed_two, axis=-1, keepdims=True)
+    )
+    grad_middle = cotangent.astype(F32) + back_two
 
     attention_gradient = flat(rows_all(grad_middle.astype(BF)))
     grad_mixed = nn(attention_gradient, weight_out).astype(BF)
@@ -401,9 +482,8 @@
         ],
         axis=1,
     )
-    attention_sums = lax.psum_scatter(
-        attention_grads, "fsdp", scatter_dimension=0, tiled=True
-    ).astype(F32)
+    attention_grads, mlp_sums = lax.optimization_barrier((attention_grads, mlp_sums))
+    attention_sums = sum_shards(attention_grads).astype(F32)
     gain_sums = lax.psum(attention_sums[:, qkv_width + query_width :], "tensor") if (
         n_tensor != 2
     ) else attention_sums[:, qkv_width + query_width :] + lax.ppermute(

time: 589 us -> 466 us (0.79)
  waiting for transfers between devices: 321 us -> 214 us
  Pallas kernels: 84.9 us -> 61.6 us
  other arithmetic: 34.9 us -> 41.3 us
    reduce_scatter x2, waiting for transfers between devices: 121 us -> 44.5 us  [sum_shards(): return lax.psum_scatter(member, 'fsdp', scatter_dimension=0, tiled=True)]
    all_gather x1, waiting for transfers between devices: 34.8 us -> 11 us  [local(): first_all = lax.all_gather(first_shard, 'fsdp', axis=0, tiled=True)]
    pallas_call x2, Pallas kernels: 84.9 us -> 61.6 us  [the longest x1 35.5 us: attend_backward(): pl.pallas_call(functools.partial(backward_kernel, group, block, grain), g...]
    ppermute x4, waiting for transfers between devices: 83.3 us -> 70.2 us  [rows_sum(): return kept + lax.ppermute(sent, 'tensor', swap).astype(F32)]
    ppermute x4, waiting for transfers between devices: 81.7 us -> 87.7 us  [rows_all(): other = lax.ppermute(member, 'tensor', swap)]
    unnamed x73 -> x83, local copies, waits for them, and re-layouts: 10.3 us -> 15.1 us
  transfers between devices with their start and end apart: 13 -> 13, of which waited for: 11 -> 11; matrix products, arithmetic and copies ran while one was open for 11% -> 21% of each run, Pallas kernels for 4% -> 13%
where the time goes in v2:
time: 466 us; the launch traced here: 461 us
  waiting for transfers between devices  214 us (46%)
  matrix products  88.1 us (19%)
  Pallas kernels  61.6 us (13%)
  other arithmetic  41.3 us (9%)
  local copies, waits for them, and re-layouts  26.4 us (6%)
  starting transfers between devices  15.8 us (3%)
  between operations  14.6 us (3%)
    ppermute x4, waiting for transfers between devices, rows_all(): other = lax.ppermute(member, 'tensor', swap)  87.7 us
    ppermute x4, waiting for transfers between devices, rows_sum(): return kept + lax.ppermute(sent, 'tensor', swap).astype(F32)  70.2 us
    reduce_scatter x2, waiting for transfers between devices, sum_shards(): return lax.psum_scatter(member, 'fsdp', scatter_dimension=0, tiled=True)  44.5 us
    dot_general x5, matrix products, nn(): return jnp.dot(left, right, preferred_element_type=F32)  36.8 us
    pallas_call x1, Pallas kernels, attend_backward(): pl.pallas_call(functools.partial(backward_kernel, group, block, grain), g...  35.5 us
    dot_general x5, matrix products, nt(): lax.dot_general(left, right, (((1,), (1,)), ((), ())), preferred_element_...  28.8 us
    pallas_call x1, Pallas kernels, attend_forward(): pl.pallas_call(functools.partial(forward_kernel, group, block, grain), gr...  26.1 us
    dot_general x5, matrix products, tn(): lax.dot_general(left, right, (((0,), (0,)), ((), ())), preferred_element_...  22.4 us
  transfers between devices with their start and end apart: 13, of which 11 were waited for; matrix products, arithmetic and copies ran while one was open for 21% of the time, Pallas kernels for 13%

profile of v2, /device:TPU:0, one launch (start us, length us, event | category | flops | bytes accessed | tf_op | source)
XLA Modules:
  0.0 461.3 jit_solution(1021705708054449452)
XLA Ops:
  14.5 3.0 collective-permute-start.1
  21.7 20.1 %collective-permute-done.1 = bf16[1,512,1024]{2,1,0:T(8,128)(2,1)} collective-permute-done((bf16[1,512,1024]{2,1,0:T(8,128)(2,1)}, bf16[1,512,1024]{2,1,0:T(8,128)(2,1)}, u32[]{:S(2)}, u32[]{:S(2)}) %collective-permute-start.1) | collective-permute-done | bytes 1048608 | tf_op jit(solution)/shard_map/ppermute | solution.py:358
  41.8 21.6 %collective-permute-done = bf16[1,512,1024]{2,1,0:T(8,128)(2,1)} collective-permute-done((bf16[1,512,1024]{2,1,0:T(8,128)(2,1)}, bf16[1,512,1024]{2,1,0:T(8,128)(2,1)}, u32[]{:S(2)}, u32[]{:S(2)}) %collective-permute-start) | collective-permute-done | bytes 1048608 | tf_op jit(solution)/shard_map/ppermute | solution.py:358
  67.6 11.0 %all-gather.3.cloned.1.call-done = bf16[1024,3200]{1,0:T(8,128)(2,1)} async-done(((bf16[64,3200]{1,0:T(8,128)(2,1)}), bf16[1024,3200]{1,0:T(8,128)(2,1)}) %all-gather.3.cloned.1.call-update) | async-done | bytes 6553616 | tf_op jit(solution)/shard_map/all_gather | solution.py:390
  82.5 6.9 %fusion.10.q_ref.k_ref.v_ref = f32[1024,2048]{1,0:T(8,128)S(1)} fusion(bf16[1024,3200]{1,0:T(8,128)(2,1)} %all-gather.3.cloned.1.call-done, bf16[1,1024,1024]{2,1,0:T(8,128)(2,1)S(1)} %pad_maximum_fusion.1, f32[1024]{0:T(1024)S(1)} %get-tuple-element.36, f32[1024]{0:T(1024)S(1)} %add_rsqrt_fusion), kind=kOutput, calls=%fused_computation.23 | convolution fusion | flops 4299161600 | bytes 14688256 | tf_op jit(solution)/shard_map/dot_general | solution.py:51
  89.4 26.1 %shard_map.237 = bf16[1024,1024]{1,0:T(8,128)(2,1)S(1)} custom-call(s32[1,4]{1,0:T(1,128)S(1)} %bitcast.75, f32[1024,2048]{1,0:T(8,128)S(1)} %fusion.10.q_ref.k_ref.v_ref, f32[1024,2048]{1,0:T(8,128)S(1)} %fusion.10.q_ref.k_ref.v_ref, f32[1024,2048]{1,0:T(8,128)S(1)} %fusion.10.q_ref.k_ref.v_ref, f32[1024,128]{1,0:T(8,128)S(1)} %get-tuple-element.72.cos_ref, ...), custom_call_target="tpu_custom_call" | custom-call | flops 2147483648 | bytes 10485760 | tf_op jit(solution)/shard_map/pallas_call | solution.py:262
  115.5 4.2 convolution_bitcast_fusion
  121.8 21.9 %collective-permute-done.2 = bf16[1,512,1024]{2,1,0:T(8,128)(2,1)S(1)} collective-permute-done((bf16[1,512,1024]{2,1,0:T(8,128)(2,1)S(1)}, bf16[1,512,1024]{2,1,0:T(8,128)(2,1)S(1)}, u32[]{:S(2)}, u32[]{:S(2)}) %collective-permute-start.2) | collective-permute-done | bytes 1048608 | tf_op jit(solution)/shard_map/ppermute | solution.py:370
  147.0 22.5 %collective-permute-done.3 = bf16[1,512,1024]{2,1,0:T(8,128)(2,1)S(1)} collective-permute-done((bf16[1,512,1024]{2,1,0:T(8,128)(2,1)S(1)}, bf16[1,512,1024]{2,1,0:T(8,128)(2,1)S(1)}, u32[]{:S(2)}, u32[]{:S(2)}) %collective-permute-start.3) | collective-permute-done | bytes 1048608 | tf_op jit(solution)/shard_map/ppermute | solution.py:358
  171.4 8.7 %fusion.12 = f32[1024,1536]{1,0:T(8,128)} fusion(bf16[1024,4608]{1,0:T(8,128)(2,1)} %all-gather.5.cloned.1.call-done, bf16[1,1024,1024]{2,1,0:T(8,128)(2,1)} %pad_maximum_fusion.2), kind=kOutput, calls=%fused_computation.28 | convolution fusion | flops 3221225472 | bytes 11534336 | tf_op jit(solution)/shard_map/dot_general | solution.py:51
  180.1 5.3 %fusion.18 = f32[1024,1536]{1,0:T(8,128)} fusion(bf16[1024,4608]{1,0:T(8,128)(2,1)S(1)} %copy-done.32, bf16[1,512,1024]{2,1,0:T(8,128)(2,1)S(1)} %copy-done.30, bf16[1,512,1024]{2,1,0:T(8,128)(2,1)S(1)} %copy-done.29), kind=kOutput, calls=%fused_computation.34 | convolution fusion | flops 3225419776 | bytes 11534336 | tf_op jit(solution)/shard_map/dot_general | solution.py:51
  185.4 11.3 %multiply_convert_fusion.1 = (bf16[1024,1536]{1,0:T(8,128)(2,1)}, bf16[1024,1536]{1,0:T(8,128)(2,1)S(1)}, bf16[1024,1536]{1,0:T(8,128)(2,1)}) fusion(f32[1024,1536]{1,0:T(8,128)} %fusion.12, f32[1024,1536]{1,0:T(8,128)} %fusion.18, bf16[1024,4608]{1,0:T(8,128)(2,1)S(1)} %copy-done.32, bf16[1,512,1024]{2,1,0:T(8,128)(2,1)S(1)} %copy-done.30, ...), kind=kOutput, calls=%fused_computation.5 | convolution fusion | flops 3249012736 | bytes 27262976 | tf_op jit(solution)/shard_map/dot_general | solution.py:51
  198.4 3.9 convolution_convert_fusion.1
  202.3 5.5 %fusion.16 = f32[1024,1024]{1,0:T(8,128)S(1)} fusion(bf16[1024,1536]{1,0:T(8,128)(2,1)} %copy-done.35, bf16[1024,4608]{1,0:T(8,128)(2,1)S(1)} %copy-done.32), kind=kOutput, calls=%fused_computation.32 | convolution fusion | flops 3221225472 | bytes 10485760 | tf_op jit(solution)/shard_map/dot_general | solution.py:47
  207.8 3.5 add_bitcast_fusion
  214.9 5.6 %convolution_convert_fusion = bf16[1024,1536]{1,0:T(8,128)(2,1)S(1)} fusion(bf16[1024,1536]{1,0:T(8,128)(2,1)} %get-tuple-element.49, bf16[1,1024,1024]{2,1,0:T(8,128)(2,1)S(1)} %copy-done.23), kind=kOutput, calls=%fused_computation.17 | convolution fusion | flops 3222798336 | bytes 8388608 | tf_op jit(solution)/shard_map/dot_general | solution.py:55
  220.5 3.8 convolution_convert_fusion.2
  224.3 5.1 %pad_maximum_fusion = bf16[1024,4608]{1,0:T(8,128)(2,1)} fusion(bf16[1024,1536]{1,0:T(8,128)(2,1)S(1)} %convolution_convert_fusion, bf16[1024,1536]{1,0:T(8,128)(2,1)S(1)} %convolution_convert_fusion.1, bf16[1024,1536]{1,0:T(8,128)(2,1)S(1)} %convolution_convert_fusion.2), kind=kLoop, calls=%fused_computation.2 | loop fusion | flops 28311552 | bytes 18874368 | tf_op jit(solution)/shard_map/concatenate | solution.py:441
  229.4 9.5 %collective-permute-done.5 = bf16[1,512,1024]{2,1,0:T(8,128)(2,1)} collective-permute-done((bf16[1,512,1024]{2,1,0:T(8,128)(2,1)}, bf16[1,512,1024]{2,1,0:T(8,128)(2,1)}, u32[]{:S(2)}, u32[]{:S(2)}) %collective-permute-start.5) | collective-permute-done | bytes 1048608 | tf_op jit(solution)/shard_map/ppermute | solution.py:370
  238.9 4.6 %convert_add_fusion.1 = f32[1,512,1024]{2,1,0:T(8,128)} fusion(bf16[1,512,1024]{2,1,0:T(8,128)(2,1)} %collective-permute-done.5, f32[1,1024,1024]{2,1,0:T(8,128)} %copy-done.17, pred[]{:T(512)S(6)} %eq.2), kind=kLoop, calls=%fused_computation.60 | loop fusion | flops 1572864 | bytes 7340033 | tf_op jit(solution)/shard_map/add | solution.py:370
  251.4 23.4 %collective-permute-done.6 = bf16[1,512,1024]{2,1,0:T(8,128)(2,1)S(1)} collective-permute-done((bf16[1,512,1024]{2,1,0:T(8,128)(2,1)S(1)}, bf16[1,512,1024]{2,1,0:T(8,128)(2,1)S(1)}, u32[]{:S(2)}, u32[]{:S(2)}) %collective-permute-start.6) | collective-permute-done | bytes 1048608 | tf_op jit(solution)/shard_map/ppermute | solution.py:358
  276.4 4.6 %convolution_convert_fusion.5.grad_ref = bf16[1024,1024]{1,0:T(8,128)(2,1)S(1)} fusion(bf16[1024,3200]{1,0:T(8,128)(2,1)} %all-gather.3.cloned.1.call-done, bf16[1,512,1024]{2,1,0:T(8,128)(2,1)S(1)} %get-tuple-element.53, bf16[1,512,1024]{2,1,0:T(8,128)(2,1)S(1)} %get-tuple-element.52), kind=kOutput, calls=%fused_computation.68 | convolution fusion | flops 2152726528 | bytes 6291456 | tf_op jit(solution)/shard_map/dot_general | solution.py:51
  281.1 35.5 %shard_map.238 = (bf16[1024,1024]{1,0:T(8,128)(2,1)S(1)}, bf16[1024,512]{1,0:T(8,128)(2,1)S(1)}, bf16[1024,512]{1,0:T(8,128)(2,1)S(1)}, f32[1,8,2,128]{3,2,1,0:T(2,128)S(1)}) custom-call(s32[1,4]{1,0:T(1,128)S(1)} %bitcast.76, f32[1024,2048]{1,0:T(8,128)S(1)} %bitcast.74, f32[1024,2048]{1,0:T(8,128)S(1)} %bitcast.74, f32[1024,2048]{1,0:T(8,128)S(1)} %bitcast.74, ...), custom_call_target="tpu_custom_call" | custom-call | flops 5368709120 | bytes 14680064 | tf_op jit(solution)/shard_map/pallas_call | solution.py:296
  323.8 10.2 %fusion.6 = (bf16[1024]{0:T(1024)(128)(2,1)S(1)}, f32[1024,1024]{1,0:T(8,128)}) fusion(bf16[1,1024,1024]{2,1,0:T(8,128)(2,1)S(1)} %copy-done.19, f32[1024]{0:T(1024)S(1)} %add_rsqrt_fusion, bf16[1024,2048]{1,0:T(8,128)(2,1)S(1)} %constant_dynamic-update-slice_fusion.4, bf16[1024,3200]{1,0:T(8,128)(2,1)} %all-gather.3.cloned.1.call-done), kind=kOutput, calls=%fused_computation.14 | convolution fusion | flops 4299160576 | bytes 14686208 | tf_op jit(solution)/shard_map/dot_general | solution.py:47
  334.3 3.8 convolution_convert_fusion.4
  338.1 5.3 %convolution_convert_fusion.3 = bf16[1024,2048]{1,0:T(8,128)(2,1)S(1)} fusion(bf16[1024,2048]{1,0:T(8,128)(2,1)S(1)} %copy-done.28, bf16[1,1024,1024]{2,1,0:T(8,128)(2,1)S(1)} %copy-done.20, f32[1024]{0:T(1024)S(1)} %get-tuple-element.36, f32[1024]{0:T(1024)S(1)} %add_rsqrt_fusion), kind=kOutput, calls=%fused_computation.20 | convolution fusion | flops 4301258752 | bytes 10493952 | tf_op jit(solution)/shard_map/dot_general | solution.py:55
  343.4 3.2 fusion.1
  346.6 8.3 %reduce-scatter.3.cloned.1.call-done = bf16[64,4608]{1,0:T(8,128)(2,1)} async-done(((bf16[1024,4608]{1,0:T(8,128)(2,1)}), bf16[64,4608]{1,0:T(8,128)(2,1)}) %reduce-scatter.3.cloned.1.call-update) | async-done | bytes 589840 | tf_op jit(solution)/shard_map/reduce_scatter | solution.py:374
  359.0 5.5 %fusion.26 = f32[1,1024,1024]{2,1,0:T(8,128)S(1)} fusion(bf16[1024,1536]{1,0:T(8,128)(2,1)S(1)} %copy-done.34, bf16[1024,4608]{1,0:T(8,128)(2,1)} %all-gather.5.cloned.1.call-done), kind=kOutput, calls=%fused_computation.42 | convolution fusion | flops 3221225472 | bytes 10485760 | tf_op jit(solution)/shard_map/dot_general | solution.py:47
  365.4 18.3 %collective-permute-done.7 = bf16[1,512,1024]{2,1,0:T(8,128)(2,1)S(1)} collective-permute-done((bf16[1,512,1024]{2,1,0:T(8,128)(2,1)S(1)}, bf16[1,512,1024]{2,1,0:T(8,128)(2,1)S(1)}, u32[]{:S(2)}, u32[]{:S(2)}) %collective-permute-start.7) | collective-permute-done | bytes 1048608 | tf_op jit(solution)/shard_map/ppermute | solution.py:370
  384.3 20.6 %collective-permute-done.4 = bf16[1,512,1024]{2,1,0:T(8,128)(2,1)S(1)} collective-permute-done((bf16[1,512,1024]{2,1,0:T(8,128)(2,1)S(1)}, bf16[1,512,1024]{2,1,0:T(8,128)(2,1)S(1)}, u32[]{:S(2)}, u32[]{:S(2)}) %collective-permute-start.4) | collective-permute-done | bytes 1048608 | tf_op jit(solution)/shard_map/ppermute | solution.py:370
  409.7 36.3 %reduce-scatter.5.cloned.1.call-done = bf16[64,3200]{1,0:T(8,128)(2,1)} async-done(((bf16[1024,3200]{1,0:T(8,128)(2,1)}), bf16[64,3200]{1,0:T(8,128)(2,1)}) %reduce-scatter.5.cloned.1.call-update) | async-done | bytes 409616 | tf_op jit(solution)/shard_map/reduce_scatter | solution.py:374
  (169 shorter events, 67.5 us)
Async XLA Ops:
  7.2 71.4 %all-gather.3.cloned.1.call-start = ((), (), s32[]{:S(2)}) async-start(), calls=%async_computation.2 | async-start | bytes 6963200 | tf_op jit(solution)/shard_map/all_gather | solution.py:390
  11.6 51.9 %copy-start.12 = (bf16[1,512,1024]{2,1,0:T(8,128)(2,1)S(1)}, bf16[1,512,1024]{2,1,0:T(8,128)(2,1)}, u32[]{:S(2)}) copy-start(bf16[1,512,1024]{2,1,0:T(8,128)(2,1)} %param.14) | copy-start | bytes 3145732
  11.6 51.9 %copy-start.15 = (bf16[1,512,1024]{2,1,0:T(8,128)(2,1)S(1)}, bf16[1,512,1024]{2,1,0:T(8,128)(2,1)}, u32[]{:S(2)}) copy-start(bf16[1,512,1024]{2,1,0:T(8,128)(2,1)} %param.27) | copy-start | bytes 3145732
  12.4 159.0 %all-gather.5.cloned.1.call-start = ((), (), s32[]{:S(2)}) async-start(), calls=%async_computation.3 | async-start | bytes 10027008 | tf_op jit(solution)/shard_map/all_gather | solution.py:391
  14.4 340.4 %reduce-scatter.3.cloned.1.call-start = ((), (), s32[]{:S(2)}) async-start(), calls=%async_computation.4 | async-start | bytes 10027008 | tf_op jit(solution)/shard_map/reduce_scatter | solution.py:374
  14.5 27.3 %collective-permute-start.1 = (bf16[1,512,1024]{2,1,0:T(8,128)(2,1)}, bf16[1,512,1024]{2,1,0:T(8,128)(2,1)}, u32[]{:S(2)}, u32[]{:S(2)}) collective-permute-start(bf16[1,512,1024]{2,1,0:T(8,128)(2,1)} %param.27), channel_id=1, source_target_pairs={{0,1},{1,0},{2,3},{3,2},{4,5},{5,4},{6,7},{7,6},{8,9},{9,8},{10,11... | collective-permute-start | bytes 3145736 | tf_op jit(solution)/shard_map/ppermute | solution.py:358
  17.5 45.9 %collective-permute-start = (bf16[1,512,1024]{2,1,0:T(8,128)(2,1)}, bf16[1,512,1024]{2,1,0:T(8,128)(2,1)}, u32[]{:S(2)}, u32[]{:S(2)}) collective-permute-start(bf16[1,512,1024]{2,1,0:T(8,128)(2,1)} %param.14), channel_id=1, source_target_pairs={{0,1},{1,0},{2,3},{3,2},{4,5},{5,4},{6,7},{7,6},{8,9},{9,8},{10,11... | collective-permute-start | bytes 3145736 | tf_op jit(solution)/shard_map/ppermute | solution.py:358
  65.5 17.0 %copy-start.18 = (bf16[1,1024,1024]{2,1,0:T(8,128)(2,1)}, bf16[1,1024,1024]{2,1,0:T(8,128)(2,1)S(1)}, u32[]{:S(2)}) copy-start(bf16[1,1024,1024]{2,1,0:T(8,128)(2,1)S(1)} %pad_maximum_fusion.1) | copy-start | bytes 6291460
  89.4 26.1 %copy-start = (f32[1024,2048]{1,0:T(8,128)}, f32[1024,2048]{1,0:T(8,128)S(1)}, u32[]{:S(2)}) copy-start(f32[1024,2048]{1,0:T(8,128)S(1)} %fusion.10.q_ref.k_ref.v_ref) | copy-start | bytes 25165828
  119.7 24.1 %copy-start.13 = (bf16[1,512,1024]{2,1,0:T(8,128)(2,1)S(1)}, bf16[1,512,1024]{2,1,0:T(8,128)(2,1)}, u32[]{:S(2)}) copy-start(bf16[1,512,1024]{2,1,0:T(8,128)(2,1)} %param.14) | copy-start | bytes 3145732
  119.9 23.9 %collective-permute-start.2 = (bf16[1,512,1024]{2,1,0:T(8,128)(2,1)S(1)}, bf16[1,512,1024]{2,1,0:T(8,128)(2,1)S(1)}, u32[]{:S(2)}, u32[]{:S(2)}) collective-permute-start(bf16[1,512,1024]{2,1,0:T(8,128)(2,1)S(1)} %select_convert_fusion.3), channel_id=1, source_target_pairs={{0,1},{1,0},{2,3},{3,2},{4,5},{5,4},{6,7},{7,6},{8,9},{9,8},{10,11... | collective-permute-start | bytes 3145736 | tf_op jit(solution)/shard_map/ppermute | solution.py:370
  144.4 25.1 %copy-start.6 = (f32[1,512,1024]{2,1,0:T(8,128)}, f32[1,512,1024]{2,1,0:T(8,128)S(1)}, u32[]{:S(2)}) copy-start(f32[1,512,1024]{2,1,0:T(8,128)S(1)} %get-tuple-element.46) | copy-start | bytes 6291460
  144.7 24.8 %collective-permute-start.3 = (bf16[1,512,1024]{2,1,0:T(8,128)(2,1)S(1)}, bf16[1,512,1024]{2,1,0:T(8,128)(2,1)S(1)}, u32[]{:S(2)}, u32[]{:S(2)}) collective-permute-start(bf16[1,512,1024]{2,1,0:T(8,128)(2,1)S(1)} %multiply_convert_fusion.3), channel_id=1, source_target_pairs={{0,1},{1,0},{2,3},{3,2},{4,5},{5,4},{6,7},{7,6},{8,9},{9,8},{10,11... | collective-permute-start | bytes 3145736 | tf_op jit(solution)/shard_map/ppermute | solution.py:358
  171.4 8.7 %copy-start.29 = (bf16[1,512,1024]{2,1,0:T(8,128)(2,1)S(1)}, bf16[1,512,1024]{2,1,0:T(8,128)(2,1)}, u32[]{:S(2)}) copy-start(bf16[1,512,1024]{2,1,0:T(8,128)(2,1)} %get-tuple-element.54) | copy-start | bytes 3145732
  171.4 8.7 %copy-start.30 = (bf16[1,512,1024]{2,1,0:T(8,128)(2,1)S(1)}, bf16[1,512,1024]{2,1,0:T(8,128)(2,1)}, u32[]{:S(2)}) copy-start(bf16[1,512,1024]{2,1,0:T(8,128)(2,1)} %get-tuple-element.55) | copy-start | bytes 3145732
  171.4 8.7 %copy-start.32 = (bf16[1024,4608]{1,0:T(8,128)(2,1)S(1)}, bf16[1024,4608]{1,0:T(8,128)(2,1)}, u32[]{:S(2)}) copy-start(bf16[1024,4608]{1,0:T(8,128)(2,1)} %all-gather.5.cloned.1.call-done) | copy-start | bytes 28311556
  211.4 9.2 %copy-start.17 = (f32[1,1024,1024]{2,1,0:T(8,128)}, f32[1,1024,1024]{2,1,0:T(8,128)S(1)}, u32[]{:S(2)}) copy-start(f32[1,1024,1024]{2,1,0:T(8,128)S(1)} %add_bitcast_fusion) | copy-start | bytes 12582916
  212.5 26.4 %collective-permute-start.5 = (bf16[1,512,1024]{2,1,0:T(8,128)(2,1)}, bf16[1,512,1024]{2,1,0:T(8,128)(2,1)}, u32[]{:S(2)}, u32[]{:S(2)}) collective-permute-start(bf16[1,512,1024]{2,1,0:T(8,128)(2,1)} %select_convert_fusion.1), channel_id=1, source_target_pairs={{0,1},{1,0},{2,3},{3,2},{4,5},{5,4},{6,7},{7,6},{8,9},{9,8},{10,11... | collective-permute-start | bytes 3145736 | tf_op jit(solution)/shard_map/ppermute | solution.py:370
  243.6 202.3 %reduce-scatter.5.cloned.1.call-start = ((), (), s32[]{:S(2)}) async-start(), calls=%async_computation.5 | async-start | bytes 6963200 | tf_op jit(solution)/shard_map/reduce_scatter | solution.py:374
  249.0 25.8 %collective-permute-start.6 = (bf16[1,512,1024]{2,1,0:T(8,128)(2,1)S(1)}, bf16[1,512,1024]{2,1,0:T(8,128)(2,1)S(1)}, u32[]{:S(2)}, u32[]{:S(2)}) collective-permute-start(bf16[1,512,1024]{2,1,0:T(8,128)(2,1)S(1)} %fusion.52), channel_id=1, source_target_pairs={{0,1},{1,0},{2,3},{3,2},{4,5},{5,4},{6,7},{7,6},{8,9},{9,8},{10,11... | collective-permute-start | bytes 3145736 | tf_op jit(solution)/shard_map/ppermute | solution.py:358
  274.8 6.3 %slice-start = ((s8[8388608]{0:T(1024)(128)(4,1)}), s8[4194304]{0:T(1024)(128)(4,1)S(1)}, s32[]{:S(2)}) async-start(s8[8388608]{0:T(1024)(128)(4,1)} %bitcast.73), calls=%async_computation.6 | async-start | bytes 8388608
  323.8 10.2 %copy-start.27 = (bf16[1024,2048]{1,0:T(8,128)(2,1)}, bf16[1024,2048]{1,0:T(8,128)(2,1)S(1)}, u32[]{:S(2)}) copy-start(bf16[1024,2048]{1,0:T(8,128)(2,1)S(1)} %constant_dynamic-update-slice_fusion.4) | copy-start | bytes 12582916
  323.8 10.4 %copy-start.25 = (bf16[1,512,1024]{2,1,0:T(8,128)(2,1)S(1)}, bf16[1,512,1024]{2,1,0:T(8,128)(2,1)}, u32[]{:S(2)}) copy-start(bf16[1,512,1024]{2,1,0:T(8,128)(2,1)} %copy-done.24) | copy-start | bytes 3145732
  357.5 26.1 %collective-permute-start.7 = (bf16[1,512,1024]{2,1,0:T(8,128)(2,1)S(1)}, bf16[1,512,1024]{2,1,0:T(8,128)(2,1)S(1)}, u32[]{:S(2)}, u32[]{:S(2)}) collective-permute-start(bf16[1,512,1024]{2,1,0:T(8,128)(2,1)S(1)} %select_convert_fusion), channel_id=1, source_target_pairs={{0,1},{1,0},{2,3},{3,2},{4,5},{5,4},{6,7},{7,6},{8,9},{9,8},{10,11... | collective-permute-start | bytes 3145736 | tf_op jit(solution)/shard_map/ppermute | solution.py:370
  359.0 24.6 %copy-start.11 = (f32[1024,1024]{1,0:T(8,128)S(1)}, f32[1024,1024]{1,0:T(8,128)}, u32[]{:S(2)}) copy-start(f32[1024,1024]{1,0:T(8,128)} %get-tuple-element.69) | copy-start | bytes 12582916
  364.5 19.1 %copy-start.14 = (bf16[1,512,1024]{2,1,0:T(8,128)(2,1)S(1)}, bf16[1,512,1024]{2,1,0:T(8,128)(2,1)}, u32[]{:S(2)}) copy-start(bf16[1,512,1024]{2,1,0:T(8,128)(2,1)} %param.14) | copy-start | bytes 3145732
  364.7 40.2 %collective-permute-start.4 = (bf16[1,512,1024]{2,1,0:T(8,128)(2,1)S(1)}, bf16[1,512,1024]{2,1,0:T(8,128)(2,1)S(1)}, u32[]{:S(2)}, u32[]{:S(2)}) collective-permute-start(bf16[1,512,1024]{2,1,0:T(8,128)(2,1)S(1)} %select_convert_fusion.2), channel_id=1, source_target_pairs={{0,1},{1,0},{2,3},{3,2},{4,5},{5,4},{6,7},{7,6},{8,9},{9,8},{10,11... | collective-permute-start | bytes 3145736 | tf_op jit(solution)/shard_map/ppermute | solution.py:370
  365.3 39.5 %copy-start.8 = (f32[1,512,1024]{2,1,0:T(8,128)S(1)}, f32[1,512,1024]{2,1,0:T(8,128)}, u32[]{:S(2)}) copy-start(f32[1,512,1024]{2,1,0:T(8,128)} %copy-done.6) | copy-start | bytes 6291460
  365.3 39.5 %copy-start.10 = (f32[1,512,1024]{2,1,0:T(8,128)S(1)}, f32[1,512,1024]{2,1,0:T(8,128)}, u32[]{:S(2)}) copy-start(f32[1,512,1024]{2,1,0:T(8,128)} %convert_add_fusion.1) | copy-start | bytes 6291460
  365.3 39.5 %copy-start.16 = (bf16[1,512,1024]{2,1,0:T(8,128)(2,1)S(1)}, bf16[1,512,1024]{2,1,0:T(8,128)(2,1)}, u32[]{:S(2)}) copy-start(bf16[1,512,1024]{2,1,0:T(8,128)(2,1)} %param.27) | copy-start | bytes 3145732
  384.3 23.6 %copy-start.22 = (bf16[64,4608]{1,0:T(8,128)(2,1)S(1)}, bf16[64,4608]{1,0:T(8,128)(2,1)}, u32[]{:S(2)}) copy-start(bf16[64,4608]{1,0:T(8,128)(2,1)} %reduce-scatter.3.cloned.1.call-done) | copy-start | bytes 1769476
  446.6 6.5 %collective-permute-start.8 = (f32[64,128]{1,0:T(8,128)S(1)}, f32[64,128]{1,0:T(8,128)S(1)}, u32[]{:S(2)}, u32[]{:S(2)}) collective-permute-start(f32[64,128]{1,0:T(8,128)S(1)} %slice.173), channel_id=1, source_target_pairs={{0,1},{1,0},{2,3},{3,2},{4,5},{5,4},{6,7},{7,6},{8,9},{9,8},{10,11... | collective-permute-start | bytes 98312 | tf_op jit(solution)/shard_map/ppermute | solution.py:489
  (19 other events, 46.7 us)
Sparse Core Ops, SparseCore 0:
  12.5 66.0 all-gather.2
  80.9 79.9 all-gather.4
  243.7 111.1 reduce-scatter.2
  359.2 86.6 reduce-scatter.4

commit v3 on v2

--- a/solution.py
+++ b/solution.py
@@ -472,23 +472,23 @@
         return jnp.pad(split, ((0, 0), (0, shard_rows - head_rows))).reshape(-1)
 
     gain_parts = jnp.stack(
-        [attn_gain_part, mlp_gain_part, spread(head_gains[0]), spread(head_gains[1])], axis=1
-    )
+        [attn_gain_part, mlp_gain_part, spread(head_gains[0]), spread(head_gains[1])]
+    )
+    if n_tensor == 2:
+        gain_parts = gain_parts + lax.ppermute(gain_parts, "tensor", swap)
+    else:
+        gain_parts = lax.psum(gain_parts, "tensor")
     attention_grads = jnp.concatenate(
         [
             tn(first_hidden, qkv_back).astype(BF),
             tn(attention_gradient, attended).astype(BF),
-            jnp.pad(gain_parts, ((0, 0), (0, LANES - 4))).astype(BF),
+            jnp.pad(gain_parts.T, ((0, 0), (0, LANES - 4))).astype(BF),
         ],
         axis=1,
     )
     attention_grads, mlp_sums = lax.optimization_barrier((attention_grads, mlp_sums))
     attention_sums = sum_shards(attention_grads).astype(F32)
-    gain_sums = lax.psum(attention_sums[:, qkv_width + query_width :], "tensor") if (
-        n_tensor != 2
-    ) else attention_sums[:, qkv_width + query_width :] + lax.ppermute(
-        attention_sums[:, qkv_width + query_width :], "tensor", swap
-    )
+    gain_sums = attention_sums[:, qkv_width + query_width :]
 
     dhidden = rows_sum(hidden_one_part)
     shaped = dhidden * gain_attn

time: 466 us -> 464 us (level)
  starting transfers between devices: 15.8 us -> 10.8 us
    unnamed x83 -> x80, local copies, waits for them, and re-layouts: 15.1 us -> 16.1 us
where the time goes in v3:
time: 464 us; the launch traced here: 458 us
  waiting for transfers between devices  212 us (46%)
  matrix products  88.2 us (19%)
  Pallas kernels  61.6 us (13%)
  other arithmetic  44.9 us (10%)
  local copies, waits for them, and re-layouts  26.4 us (6%)
  between operations  14.5 us (3%)
  starting transfers between devices  10.8 us (2%)
    ppermute x4, waiting for transfers between devices, rows_all(): other = lax.ppermute(member, 'tensor', swap)  87.2 us
    ppermute x4, waiting for transfers between devices, rows_sum(): return kept + lax.ppermute(sent, 'tensor', swap).astype(F32)  70.4 us
    reduce_scatter x2, waiting for transfers between devices, sum_shards(): return lax.psum_scatter(member, 'fsdp', scatter_dimension=0, tiled=True)  43.1 us
    dot_general x5, matrix products, nn(): return jnp.dot(left, right, preferred_element_type=F32)  37.3 us
    pallas_call x1, Pallas kernels, attend_backward(): pl.pallas_call(functools.partial(backward_kernel, group, block, grain), g...  35.5 us
    dot_general x5, matrix products, nt(): lax.dot_general(left, right, (((1,), (1,)), ((), ())), preferred_element_...  27.1 us
    pallas_call x1, Pallas kernels, attend_forward(): pl.pallas_call(functools.partial(forward_kernel, group, block, grain), gr...  26.1 us
    dot_general x5, matrix products, tn(): lax.dot_general(left, right, (((0,), (0,)), ((), ())), preferred_element_...  23.7 us
  transfers between devices with their start and end apart: 13, of which 11 were waited for; matrix products, arithmetic and copies ran while one was open for 21% of the time, Pallas kernels for 13%

profile of v3, /device:TPU:0, one launch (start us, length us, event | category | flops | bytes accessed | tf_op | source)
XLA Modules:
  0.0 458.1 jit_solution(13565548230051264247)
XLA Ops:
  14.5 3.0 collective-permute-start.1
  21.7 20.1 %collective-permute-done.1 = bf16[1,512,1024]{2,1,0:T(8,128)(2,1)} collective-permute-done((bf16[1,512,1024]{2,1,0:T(8,128)(2,1)}, bf16[1,512,1024]{2,1,0:T(8,128)(2,1)}, u32[]{:S(2)}, u32[]{:S(2)}) %collective-permute-start.1) | collective-permute-done | bytes 1048608 | tf_op jit(solution)/shard_map/ppermute | solution.py:358
  41.8 21.6 %collective-permute-done = bf16[1,512,1024]{2,1,0:T(8,128)(2,1)} collective-permute-done((bf16[1,512,1024]{2,1,0:T(8,128)(2,1)}, bf16[1,512,1024]{2,1,0:T(8,128)(2,1)}, u32[]{:S(2)}, u32[]{:S(2)}) %collective-permute-start) | collective-permute-done | bytes 1048608 | tf_op jit(solution)/shard_map/ppermute | solution.py:358
  67.6 11.0 %all-gather.3.cloned.1.call-done = bf16[1024,3200]{1,0:T(8,128)(2,1)} async-done(((bf16[64,3200]{1,0:T(8,128)(2,1)}), bf16[1024,3200]{1,0:T(8,128)(2,1)}) %all-gather.3.cloned.1.call-update) | async-done | bytes 6553616 | tf_op jit(solution)/shard_map/all_gather | solution.py:390
  82.5 6.9 %fusion.10.q_ref.k_ref.v_ref = f32[1024,2048]{1,0:T(8,128)S(1)} fusion(bf16[1024,3200]{1,0:T(8,128)(2,1)} %all-gather.3.cloned.1.call-done, bf16[1,1024,1024]{2,1,0:T(8,128)(2,1)S(1)} %pad_maximum_fusion.1, f32[1024]{0:T(1024)S(1)} %get-tuple-element.40, f32[1024]{0:T(1024)S(1)} %add_rsqrt_fusion), kind=kOutput, calls=%fused_computation.23 | convolution fusion | flops 4299161600 | bytes 14688256 | tf_op jit(solution)/shard_map/dot_general | solution.py:51
  89.4 26.1 %shard_map.237 = bf16[1024,1024]{1,0:T(8,128)(2,1)S(1)} custom-call(s32[1,4]{1,0:T(1,128)S(1)} %bitcast.79, f32[1024,2048]{1,0:T(8,128)S(1)} %fusion.10.q_ref.k_ref.v_ref, f32[1024,2048]{1,0:T(8,128)S(1)} %fusion.10.q_ref.k_ref.v_ref, f32[1024,2048]{1,0:T(8,128)S(1)} %fusion.10.q_ref.k_ref.v_ref, f32[1024,128]{1,0:T(8,128)S(1)} %get-tuple-element.72.cos_ref, ...), custom_call_target="tpu_custom_call" | custom-call | flops 2147483648 | bytes 10485760 | tf_op jit(solution)/shard_map/pallas_call | solution.py:262
  115.5 4.3 convolution_bitcast_fusion
  121.8 23.8 %collective-permute-done.2 = bf16[1,512,1024]{2,1,0:T(8,128)(2,1)S(1)} collective-permute-done((bf16[1,512,1024]{2,1,0:T(8,128)(2,1)S(1)}, bf16[1,512,1024]{2,1,0:T(8,128)(2,1)S(1)}, u32[]{:S(2)}, u32[]{:S(2)}) %collective-permute-start.2) | collective-permute-done | bytes 1048608 | tf_op jit(solution)/shard_map/ppermute | solution.py:370
  148.2 23.3 %collective-permute-done.3 = bf16[1,512,1024]{2,1,0:T(8,128)(2,1)S(1)} collective-permute-done((bf16[1,512,1024]{2,1,0:T(8,128)(2,1)S(1)}, bf16[1,512,1024]{2,1,0:T(8,128)(2,1)S(1)}, u32[]{:S(2)}, u32[]{:S(2)}) %collective-permute-start.3) | collective-permute-done | bytes 1048608 | tf_op jit(solution)/shard_map/ppermute | solution.py:358
  173.4 8.7 %fusion.12 = f32[1024,1536]{1,0:T(8,128)} fusion(bf16[1024,4608]{1,0:T(8,128)(2,1)} %all-gather.5.cloned.1.call-done, bf16[1,1024,1024]{2,1,0:T(8,128)(2,1)} %pad_maximum_fusion.2), kind=kOutput, calls=%fused_computation.28 | convolution fusion | flops 3221225472 | bytes 11534336 | tf_op jit(solution)/shard_map/dot_general | solution.py:51
  182.1 5.3 %fusion.18 = f32[1024,1536]{1,0:T(8,128)} fusion(bf16[1024,4608]{1,0:T(8,128)(2,1)S(1)} %copy-done.30, bf16[1,512,1024]{2,1,0:T(8,128)(2,1)S(1)} %copy-done.28, bf16[1,512,1024]{2,1,0:T(8,128)(2,1)S(1)} %copy-done.27), kind=kOutput, calls=%fused_computation.34 | convolution fusion | flops 3225419776 | bytes 11534336 | tf_op jit(solution)/shard_map/dot_general | solution.py:51
  187.4 11.3 %multiply_convert_fusion.1 = (bf16[1024,1536]{1,0:T(8,128)(2,1)}, bf16[1024,1536]{1,0:T(8,128)(2,1)S(1)}, bf16[1024,1536]{1,0:T(8,128)(2,1)}) fusion(f32[1024,1536]{1,0:T(8,128)} %fusion.12, f32[1024,1536]{1,0:T(8,128)} %fusion.18, bf16[1024,4608]{1,0:T(8,128)(2,1)S(1)} %copy-done.30, bf16[1,512,1024]{2,1,0:T(8,128)(2,1)S(1)} %copy-done.28, ...), kind=kOutput, calls=%fused_computation.5 | convolution fusion | flops 3249012736 | bytes 27262976 | tf_op jit(solution)/shard_map/dot_general | solution.py:51
  200.4 3.9 convolution_convert_fusion.1
  204.4 5.5 %fusion.16 = f32[1024,1024]{1,0:T(8,128)S(1)} fusion(bf16[1024,1536]{1,0:T(8,128)(2,1)} %copy-done.33, bf16[1024,4608]{1,0:T(8,128)(2,1)S(1)} %copy-done.30), kind=kOutput, calls=%fused_computation.32 | convolution fusion | flops 3221225472 | bytes 10485760 | tf_op jit(solution)/shard_map/dot_general | solution.py:47
  209.8 3.5 add_bitcast_fusion
  216.5 5.6 %convolution_convert_fusion = bf16[1024,1536]{1,0:T(8,128)(2,1)S(1)} fusion(bf16[1024,1536]{1,0:T(8,128)(2,1)} %get-tuple-element.49, bf16[1,1024,1024]{2,1,0:T(8,128)(2,1)S(1)} %copy-done.22), kind=kOutput, calls=%fused_computation.17 | convolution fusion | flops 3222798336 | bytes 8388608 | tf_op jit(solution)/shard_map/dot_general | solution.py:55
  222.2 3.8 convolution_convert_fusion.2
  226.0 5.1 %pad_maximum_fusion = bf16[1024,4608]{1,0:T(8,128)(2,1)} fusion(bf16[1024,1536]{1,0:T(8,128)(2,1)S(1)} %convolution_convert_fusion, bf16[1024,1536]{1,0:T(8,128)(2,1)S(1)} %convolution_convert_fusion.1, bf16[1024,1536]{1,0:T(8,128)(2,1)S(1)} %convolution_convert_fusion.2), kind=kLoop, calls=%fused_computation.2 | loop fusion | flops 28311552 | bytes 18874368 | tf_op jit(solution)/shard_map/concatenate | solution.py:441
  231.1 7.8 %collective-permute-done.5 = bf16[1,512,1024]{2,1,0:T(8,128)(2,1)} collective-permute-done((bf16[1,512,1024]{2,1,0:T(8,128)(2,1)}, bf16[1,512,1024]{2,1,0:T(8,128)(2,1)}, u32[]{:S(2)}, u32[]{:S(2)}) %collective-permute-start.5) | collective-permute-done | bytes 1048608 | tf_op jit(solution)/shard_map/ppermute | solution.py:370
  238.8 4.6 %convert_add_fusion.1 = f32[1,512,1024]{2,1,0:T(8,128)} fusion(bf16[1,512,1024]{2,1,0:T(8,128)(2,1)} %collective-permute-done.5, f32[1,1024,1024]{2,1,0:T(8,128)} %copy-done.17, pred[]{:T(512)S(6)} %eq.2), kind=kLoop, calls=%fused_computation.60 | loop fusion | flops 1572864 | bytes 7340033 | tf_op jit(solution)/shard_map/add | solution.py:370
  249.8 22.2 %collective-permute-done.6 = bf16[1,512,1024]{2,1,0:T(8,128)(2,1)S(1)} collective-permute-done((bf16[1,512,1024]{2,1,0:T(8,128)(2,1)S(1)}, bf16[1,512,1024]{2,1,0:T(8,128)(2,1)S(1)}, u32[]{:S(2)}, u32[]{:S(2)}) %collective-permute-start.6) | collective-permute-done | bytes 1048608 | tf_op jit(solution)/shard_map/ppermute | solution.py:358
  273.6 5.1 %convolution_convert_fusion.5.grad_ref = bf16[1024,1024]{1,0:T(8,128)(2,1)S(1)} fusion(bf16[1024,3200]{1,0:T(8,128)(2,1)} %all-gather.3.cloned.1.call-done, bf16[1,512,1024]{2,1,0:T(8,128)(2,1)S(1)} %get-tuple-element.53, bf16[1,512,1024]{2,1,0:T(8,128)(2,1)S(1)} %get-tuple-element.52), kind=kOutput, calls=%fused_computation.68 | convolution fusion | flops 2152726528 | bytes 6291456 | tf_op jit(solution)/shard_map/dot_general | solution.py:51
  278.8 35.5 %shard_map.238 = (bf16[1024,1024]{1,0:T(8,128)(2,1)S(1)}, bf16[1024,512]{1,0:T(8,128)(2,1)S(1)}, bf16[1024,512]{1,0:T(8,128)(2,1)S(1)}, f32[1,8,2,128]{3,2,1,0:T(2,128)S(1)}) custom-call(s32[1,4]{1,0:T(1,128)S(1)} %bitcast.80, f32[1024,2048]{1,0:T(8,128)S(1)} %bitcast.78, f32[1024,2048]{1,0:T(8,128)S(1)} %bitcast.78, f32[1024,2048]{1,0:T(8,128)S(1)} %bitcast.78, ...), custom_call_target="tpu_custom_call" | custom-call | flops 5368709120 | bytes 14680064 | tf_op jit(solution)/shard_map/pallas_call | solution.py:296
  321.5 8.4 %fusion.6 = (f32[1024]{0:T(1024)S(1)}, f32[1024,1024]{1,0:T(8,128)}) fusion(bf16[1,1024,1024]{2,1,0:T(8,128)(2,1)S(1)} %copy-done.19, f32[1024]{0:T(1024)S(1)} %add_rsqrt_fusion, bf16[1024,2048]{1,0:T(8,128)(2,1)S(1)} %constant_dynamic-update-slice_fusion.4, bf16[1024,3200]{1,0:T(8,128)(2,1)} %all-gather.3.cloned.1.call-done), kind=kOutput, calls=%fused_computation.14 | convolution fusion | flops 4299160576 | bytes 14688256 | tf_op jit(solution)/shard_map/dot_general | solution.py:47
  330.0 6.6 %convolution_convert_fusion.3 = bf16[1024,2048]{1,0:T(8,128)(2,1)} fusion(bf16[1024,2048]{1,0:T(8,128)(2,1)S(1)} %constant_dynamic-update-slice_fusion.4, bf16[1,1024,1024]{2,1,0:T(8,128)(2,1)S(1)} %copy-done.19, f32[1024]{0:T(1024)S(1)} %get-tuple-element.40, f32[1024]{0:T(1024)S(1)} %add_rsqrt_fusion), kind=kOutput, calls=%fused_computation.20 | convolution fusion | flops 4301258752 | bytes 10493952 | tf_op jit(solution)/shard_map/dot_general | solution.py:55
  336.6 3.8 convolution_convert_fusion.4
  340.6 6.5 %fusion.1 = bf16[1024,3200]{1,0:T(8,128)(2,1)} fusion(bf16[1024,4]{1,0:T(8,128)(2,1)S(1)} %copy.54, bf16[1024,1024]{1,0:T(8,128)(2,1)} %convolution_convert_fusion.4, bf16[1024,2048]{1,0:T(8,128)(2,1)} %convolution_convert_fusion.3), kind=kLoop, calls=%fused_computation.3 | loop fusion | flops 26214400 | bytes 12853248 | tf_op jit(solution)/shard_map/concatenate | solution.py:481
  347.1 6.8 %reduce-scatter.3.cloned.1.call-done = bf16[64,4608]{1,0:T(8,128)(2,1)} async-done(((bf16[1024,4608]{1,0:T(8,128)(2,1)}), bf16[64,4608]{1,0:T(8,128)(2,1)}) %reduce-scatter.3.cloned.1.call-update) | async-done | bytes 589840 | tf_op jit(solution)/shard_map/reduce_scatter | solution.py:374
  358.1 5.5 %fusion.26 = f32[1,1024,1024]{2,1,0:T(8,128)S(1)} fusion(bf16[1024,1536]{1,0:T(8,128)(2,1)S(1)} %copy-done.32, bf16[1024,4608]{1,0:T(8,128)(2,1)} %all-gather.5.cloned.1.call-done), kind=kOutput, calls=%fused_computation.42 | convolution fusion | flops 3221225472 | bytes 10485760 | tf_op jit(solution)/shard_map/dot_general | solution.py:47
  364.4 18.3 %collective-permute-done.7 = bf16[1,512,1024]{2,1,0:T(8,128)(2,1)S(1)} collective-permute-done((bf16[1,512,1024]{2,1,0:T(8,128)(2,1)S(1)}, bf16[1,512,1024]{2,1,0:T(8,128)(2,1)S(1)}, u32[]{:S(2)}, u32[]{:S(2)}) %collective-permute-start.7) | collective-permute-done | bytes 1048608 | tf_op jit(solution)/shard_map/ppermute | solution.py:370
  383.4 20.6 %collective-permute-done.4 = bf16[1,512,1024]{2,1,0:T(8,128)(2,1)S(1)} collective-permute-done((bf16[1,512,1024]{2,1,0:T(8,128)(2,1)S(1)}, bf16[1,512,1024]{2,1,0:T(8,128)(2,1)S(1)}, u32[]{:S(2)}, u32[]{:S(2)}) %collective-permute-start.4) | collective-permute-done | bytes 1048608 | tf_op jit(solution)/shard_map/ppermute | solution.py:370
  408.8 36.2 %reduce-scatter.5.cloned.1.call-done = bf16[64,3200]{1,0:T(8,128)(2,1)} async-done(((bf16[1024,3200]{1,0:T(8,128)(2,1)}), bf16[64,3200]{1,0:T(8,128)(2,1)}) %reduce-scatter.5.cloned.1.call-update) | async-done | bytes 409616 | tf_op jit(solution)/shard_map/reduce_scatter | solution.py:374
  (162 shorter events, 62.9 us)
Async XLA Ops:
  7.2 71.4 %all-gather.3.cloned.1.call-start = ((), (), s32[]{:S(2)}) async-start(), calls=%async_computation.2 | async-start | bytes 6963200 | tf_op jit(solution)/shard_map/all_gather | solution.py:390
  11.6 51.9 %copy-start.12 = (bf16[1,512,1024]{2,1,0:T(8,128)(2,1)S(1)}, bf16[1,512,1024]{2,1,0:T(8,128)(2,1)}, u32[]{:S(2)}) copy-start(bf16[1,512,1024]{2,1,0:T(8,128)(2,1)} %param.14) | copy-start | bytes 3145732
  11.6 51.9 %copy-start.15 = (bf16[1,512,1024]{2,1,0:T(8,128)(2,1)S(1)}, bf16[1,512,1024]{2,1,0:T(8,128)(2,1)}, u32[]{:S(2)}) copy-start(bf16[1,512,1024]{2,1,0:T(8,128)(2,1)} %param.27) | copy-start | bytes 3145732
  12.4 161.0 %all-gather.5.cloned.1.call-start = ((), (), s32[]{:S(2)}) async-start(), calls=%async_computation.3 | async-start | bytes 10027008 | tf_op jit(solution)/shard_map/all_gather | solution.py:391
  14.4 339.5 %reduce-scatter.3.cloned.1.call-start = ((), (), s32[]{:S(2)}) async-start(), calls=%async_computation.4 | async-start | bytes 10027008 | tf_op jit(solution)/shard_map/reduce_scatter | solution.py:374
  14.5 27.3 %collective-permute-start.1 = (bf16[1,512,1024]{2,1,0:T(8,128)(2,1)}, bf16[1,512,1024]{2,1,0:T(8,128)(2,1)}, u32[]{:S(2)}, u32[]{:S(2)}) collective-permute-start(bf16[1,512,1024]{2,1,0:T(8,128)(2,1)} %param.27), channel_id=1, source_target_pairs={{0,1},{1,0},{2,3},{3,2},{4,5},{5,4},{6,7},{7,6},{8,9},{9,8},{10,11... | collective-permute-start | bytes 3145736 | tf_op jit(solution)/shard_map/ppermute | solution.py:358
  17.5 45.9 %collective-permute-start = (bf16[1,512,1024]{2,1,0:T(8,128)(2,1)}, bf16[1,512,1024]{2,1,0:T(8,128)(2,1)}, u32[]{:S(2)}, u32[]{:S(2)}) collective-permute-start(bf16[1,512,1024]{2,1,0:T(8,128)(2,1)} %param.14), channel_id=1, source_target_pairs={{0,1},{1,0},{2,3},{3,2},{4,5},{5,4},{6,7},{7,6},{8,9},{9,8},{10,11... | collective-permute-start | bytes 3145736 | tf_op jit(solution)/shard_map/ppermute | solution.py:358
  65.5 17.0 %copy-start.18 = (bf16[1,1024,1024]{2,1,0:T(8,128)(2,1)}, bf16[1,1024,1024]{2,1,0:T(8,128)(2,1)S(1)}, u32[]{:S(2)}) copy-start(bf16[1,1024,1024]{2,1,0:T(8,128)(2,1)S(1)} %pad_maximum_fusion.1) | copy-start | bytes 6291460
  89.4 26.1 %copy-start = (f32[1024,2048]{1,0:T(8,128)}, f32[1024,2048]{1,0:T(8,128)S(1)}, u32[]{:S(2)}) copy-start(f32[1024,2048]{1,0:T(8,128)S(1)} %fusion.10.q_ref.k_ref.v_ref) | copy-start | bytes 25165828
  119.8 25.9 %copy-start.13 = (bf16[1,512,1024]{2,1,0:T(8,128)(2,1)S(1)}, bf16[1,512,1024]{2,1,0:T(8,128)(2,1)}, u32[]{:S(2)}) copy-start(bf16[1,512,1024]{2,1,0:T(8,128)(2,1)} %param.14) | copy-start | bytes 3145732
  120.0 25.7 %collective-permute-start.2 = (bf16[1,512,1024]{2,1,0:T(8,128)(2,1)S(1)}, bf16[1,512,1024]{2,1,0:T(8,128)(2,1)S(1)}, u32[]{:S(2)}, u32[]{:S(2)}) collective-permute-start(bf16[1,512,1024]{2,1,0:T(8,128)(2,1)S(1)} %select_convert_fusion.3), channel_id=1, source_target_pairs={{0,1},{1,0},{2,3},{3,2},{4,5},{5,4},{6,7},{7,6},{8,9},{9,8},{10,11... | collective-permute-start | bytes 3145736 | tf_op jit(solution)/shard_map/ppermute | solution.py:370
  146.4 25.2 %copy-start.6 = (f32[1,512,1024]{2,1,0:T(8,128)}, f32[1,512,1024]{2,1,0:T(8,128)S(1)}, u32[]{:S(2)}) copy-start(f32[1,512,1024]{2,1,0:T(8,128)S(1)} %get-tuple-element.46) | copy-start | bytes 6291460
  146.6 24.9 %collective-permute-start.3 = (bf16[1,512,1024]{2,1,0:T(8,128)(2,1)S(1)}, bf16[1,512,1024]{2,1,0:T(8,128)(2,1)S(1)}, u32[]{:S(2)}, u32[]{:S(2)}) collective-permute-start(bf16[1,512,1024]{2,1,0:T(8,128)(2,1)S(1)} %multiply_convert_fusion.3), channel_id=1, source_target_pairs={{0,1},{1,0},{2,3},{3,2},{4,5},{5,4},{6,7},{7,6},{8,9},{9,8},{10,11... | collective-permute-start | bytes 3145736 | tf_op jit(solution)/shard_map/ppermute | solution.py:358
  173.4 8.7 %copy-start.27 = (bf16[1,512,1024]{2,1,0:T(8,128)(2,1)S(1)}, bf16[1,512,1024]{2,1,0:T(8,128)(2,1)}, u32[]{:S(2)}) copy-start(bf16[1,512,1024]{2,1,0:T(8,128)(2,1)} %get-tuple-element.54) | copy-start | bytes 3145732
  173.4 8.7 %copy-start.28 = (bf16[1,512,1024]{2,1,0:T(8,128)(2,1)S(1)}, bf16[1,512,1024]{2,1,0:T(8,128)(2,1)}, u32[]{:S(2)}) copy-start(bf16[1,512,1024]{2,1,0:T(8,128)(2,1)} %get-tuple-element.55) | copy-start | bytes 3145732
  173.4 8.7 %copy-start.30 = (bf16[1024,4608]{1,0:T(8,128)(2,1)S(1)}, bf16[1024,4608]{1,0:T(8,128)(2,1)}, u32[]{:S(2)}) copy-start(bf16[1024,4608]{1,0:T(8,128)(2,1)} %all-gather.5.cloned.1.call-done) | copy-start | bytes 28311556
  213.4 8.8 %copy-start.17 = (f32[1,1024,1024]{2,1,0:T(8,128)}, f32[1,1024,1024]{2,1,0:T(8,128)S(1)}, u32[]{:S(2)}) copy-start(f32[1,1024,1024]{2,1,0:T(8,128)S(1)} %add_bitcast_fusion) | copy-start | bytes 12582916
  214.5 24.3 %collective-permute-start.5 = (bf16[1,512,1024]{2,1,0:T(8,128)(2,1)}, bf16[1,512,1024]{2,1,0:T(8,128)(2,1)}, u32[]{:S(2)}, u32[]{:S(2)}) collective-permute-start(bf16[1,512,1024]{2,1,0:T(8,128)(2,1)} %select_convert_fusion.1), channel_id=1, source_target_pairs={{0,1},{1,0},{2,3},{3,2},{4,5},{5,4},{6,7},{7,6},{8,9},{9,8},{10,11... | collective-permute-start | bytes 3145736 | tf_op jit(solution)/shard_map/ppermute | solution.py:370
  243.5 201.5 %reduce-scatter.5.cloned.1.call-start = ((), (), s32[]{:S(2)}) async-start(), calls=%async_computation.5 | async-start | bytes 6963200 | tf_op jit(solution)/shard_map/reduce_scatter | solution.py:374
  249.2 22.8 %collective-permute-start.6 = (bf16[1,512,1024]{2,1,0:T(8,128)(2,1)S(1)}, bf16[1,512,1024]{2,1,0:T(8,128)(2,1)S(1)}, u32[]{:S(2)}, u32[]{:S(2)}) collective-permute-start(bf16[1,512,1024]{2,1,0:T(8,128)(2,1)S(1)} %fusion.53), channel_id=1, source_target_pairs={{0,1},{1,0},{2,3},{3,2},{4,5},{5,4},{6,7},{7,6},{8,9},{9,8},{10,11... | collective-permute-start | bytes 3145736 | tf_op jit(solution)/shard_map/ppermute | solution.py:358
  272.0 6.8 %slice-start = ((s8[8388608]{0:T(1024)(128)(4,1)}), s8[4194304]{0:T(1024)(128)(4,1)S(1)}, s32[]{:S(2)}) async-start(s8[8388608]{0:T(1024)(128)(4,1)} %bitcast.77), calls=%async_computation.6 | async-start | bytes 8388608
  329.9 6.7 %copy-start.24 = (bf16[1,512,1024]{2,1,0:T(8,128)(2,1)S(1)}, bf16[1,512,1024]{2,1,0:T(8,128)(2,1)}, u32[]{:S(2)}) copy-start(bf16[1,512,1024]{2,1,0:T(8,128)(2,1)} %copy-done.23) | copy-start | bytes 3145732
  329.9 6.7 %copy-start.26 = (bf16[1,512,1024]{2,1,0:T(8,128)(2,1)S(1)}, bf16[1,512,1024]{2,1,0:T(8,128)(2,1)}, u32[]{:S(2)}) copy-start(bf16[1,512,1024]{2,1,0:T(8,128)(2,1)} %copy-done.25) | copy-start | bytes 3145732
  329.9 10.5 %collective-permute-start.8 = (f32[4,1024]{1,0:T(4,128)S(1)}, f32[4,1024]{1,0:T(4,128)S(1)}, u32[]{:S(2)}, u32[]{:S(2)}) collective-permute-start(f32[4,1024]{1,0:T(4,128)S(1)} %pad_maximum_fusion.4), channel_id=1, source_target_pairs={{0,1},{1,0},{2,3},{3,2},{4,5},{5,4},{6,7},{7,6},{8,9},{9,8},{10,11... | collective-permute-start | bytes 49160 | tf_op jit(solution)/shard_map/ppermute | solution.py:478
  356.6 26.1 %collective-permute-start.7 = (bf16[1,512,1024]{2,1,0:T(8,128)(2,1)S(1)}, bf16[1,512,1024]{2,1,0:T(8,128)(2,1)S(1)}, u32[]{:S(2)}, u32[]{:S(2)}) collective-permute-start(bf16[1,512,1024]{2,1,0:T(8,128)(2,1)S(1)} %select_convert_fusion), channel_id=1, source_target_pairs={{0,1},{1,0},{2,3},{3,2},{4,5},{5,4},{6,7},{7,6},{8,9},{9,8},{10,11... | collective-permute-start | bytes 3145736 | tf_op jit(solution)/shard_map/ppermute | solution.py:370
  358.1 24.6 %copy-start.11 = (f32[1024,1024]{1,0:T(8,128)S(1)}, f32[1024,1024]{1,0:T(8,128)}, u32[]{:S(2)}) copy-start(f32[1024,1024]{1,0:T(8,128)} %get-tuple-element.69) | copy-start | bytes 12582916
  363.6 19.1 %copy-start.14 = (bf16[1,512,1024]{2,1,0:T(8,128)(2,1)S(1)}, bf16[1,512,1024]{2,1,0:T(8,128)(2,1)}, u32[]{:S(2)}) copy-start(bf16[1,512,1024]{2,1,0:T(8,128)(2,1)} %param.14) | copy-start | bytes 3145732
  363.8 40.2 %collective-permute-start.4 = (bf16[1,512,1024]{2,1,0:T(8,128)(2,1)S(1)}, bf16[1,512,1024]{2,1,0:T(8,128)(2,1)S(1)}, u32[]{:S(2)}, u32[]{:S(2)}) collective-permute-start(bf16[1,512,1024]{2,1,0:T(8,128)(2,1)S(1)} %select_convert_fusion.2), channel_id=1, source_target_pairs={{0,1},{1,0},{2,3},{3,2},{4,5},{5,4},{6,7},{7,6},{8,9},{9,8},{10,11... | collective-permute-start | bytes 3145736 | tf_op jit(solution)/shard_map/ppermute | solution.py:370
  364.4 39.5 %copy-start.8 = (f32[1,512,1024]{2,1,0:T(8,128)S(1)}, f32[1,512,1024]{2,1,0:T(8,128)}, u32[]{:S(2)}) copy-start(f32[1,512,1024]{2,1,0:T(8,128)} %copy-done.6) | copy-start | bytes 6291460
  364.4 39.5 %copy-start.10 = (f32[1,512,1024]{2,1,0:T(8,128)S(1)}, f32[1,512,1024]{2,1,0:T(8,128)}, u32[]{:S(2)}) copy-start(f32[1,512,1024]{2,1,0:T(8,128)} %convert_add_fusion.1) | copy-start | bytes 6291460
  364.4 39.5 %copy-start.16 = (bf16[1,512,1024]{2,1,0:T(8,128)(2,1)S(1)}, bf16[1,512,1024]{2,1,0:T(8,128)(2,1)}, u32[]{:S(2)}) copy-start(bf16[1,512,1024]{2,1,0:T(8,128)(2,1)} %param.27) | copy-start | bytes 3145732
  383.4 23.6 %copy-start.21 = (bf16[64,4608]{1,0:T(8,128)(2,1)S(1)}, bf16[64,4608]{1,0:T(8,128)(2,1)}, u32[]{:S(2)}) copy-start(bf16[64,4608]{1,0:T(8,128)(2,1)} %reduce-scatter.3.cloned.1.call-done) | copy-start | bytes 1769476
  (17 other events, 39.2 us)
Sparse Core Ops, SparseCore 0:
  12.5 66.0 all-gather.2
  80.9 79.9 all-gather.4
  243.6 110.3 reduce-scatter.2
  358.3 86.6 reduce-scatter.4
